TPU v7x, 128 devices: a whole 4x4x4 slice. The times are simulated.
128 devices in a mesh: seq: 16 (over x, z), roll: 2 (over y_lo), head: 4 (over y_hi, core).
Axes of the slice: x: 4, y: 4 (y_hi: 2, y_lo: 2; y = y_hi * 2 + y_lo), z: 4, core: 2. Of those that a mesh axis runs over, the one named last changes fastest.
Arguments:
- queries: bfloat16 [2, 3072, 64, 128], P('roll', 'seq', 'head'), may hold values from -7 to 7
- rollout_keys: bfloat16 [2, 3072, 8, 128], P('roll', 'seq', 'head'), may hold values from -6 to 6
- rollout_values: bfloat16 [2, 3072, 8, 128], P('roll', 'seq', 'head'), may hold values from -24 to 24
- prompt_keys: bfloat16 [1024, 8, 128], P(('seq', 'roll'), 'head'), may hold values from -4.5 to 4.5
- prompt_values: bfloat16 [1024, 8, 128], P(('seq', 'roll'), 'head'), may hold values from -24 to 24
- grad_out: bfloat16 [2, 3072, 64, 128], P('roll', 'seq', 'head'), may hold values from -24 to 24
- lengths: int32 [2], P('roll'), may hold values from 768 to 3072, as said below
Outputs:
- attention_out: bfloat16 [2, 3072, 64, 128], P('roll', 'seq', 'head')
- grad_queries: bfloat16 [2, 3072, 64, 128], P('roll', 'seq', 'head')
- grad_rollout_keys: bfloat16 [2, 3072, 8, 128], P('roll', 'seq', 'head')
- grad_rollout_values: bfloat16 [2, 3072, 8, 128], P('roll', 'seq', 'head')
- grad_prompt_keys: bfloat16 [1024, 8, 128], P(('seq', 'roll'), 'head')
- grad_prompt_values: bfloat16 [1024, 8, 128], P(('seq', 'roll'), 'head')
Inputs may be any that keep to these rules, and one draw needn't show every extreme that they name: `lengths`: every rollout's length is at least 768, and one rollout of each draw has all 3072 positions live.
All inputs are finite; a program needn't handle non-finite values.
Results may differ from a plain program's by a relative error of at most 0.007.
Values may be sent and summed in bfloat16 or wider, within the bound.
A program may use at most 128 MiB of HBM per device.

v0:
```python
import math

import jax
import jax.numpy as jnp
from jax import lax
from jax.sharding import PartitionSpec as P


def scores_for(query_grid, key_block, key_pos, query_pos, score_scale):
    scores = (
        jnp.einsum("ngqd,kgd->gqnk", query_grid, key_block, preferred_element_type=jnp.float32)
        * score_scale
    )
    allowed = key_pos[None, :] <= query_pos[:, None]
    return jnp.where(allowed[None, None], scores, -jnp.inf)


def max_block(maxima, query_grid, key_block, key_pos, query_pos, score_scale):
    scores = scores_for(query_grid, key_block, key_pos, query_pos, score_scale)
    return jnp.maximum(maxima, jnp.max(scores, -1))


def forward_block(
    running, maxima, query_grid, key_block, value_block, key_pos, query_pos, score_scale
):
    totals, summed = running
    scores = scores_for(query_grid, key_block, key_pos, query_pos, score_scale)
    lifted = jnp.exp(scores - maxima[..., None])
    totals = totals + jnp.sum(lifted, -1)
    summed = summed + jnp.einsum(
        "gqnk,kgd->gqnd",
        lifted.astype(jnp.bfloat16),
        value_block,
        preferred_element_type=jnp.float32,
    )
    return (totals, summed)


def score_grads(
    query_grid,
    cot_grid,
    key_block,
    value_block,
    key_pos,
    query_pos,
    log_total,
    offsets,
    score_scale,
):
    scores = scores_for(query_grid, key_block, key_pos, query_pos, score_scale)
    weights = jnp.exp(scores - log_total[..., None])
    grad_weights = jnp.einsum(
        "ngqd,kgd->gqnk", cot_grid, value_block, preferred_element_type=jnp.float32
    )
    grad_scores = (weights * (grad_weights - offsets[..., None]) * score_scale).astype(jnp.bfloat16)
    return (grad_scores, weights.astype(jnp.bfloat16))


def backward_block(
    query_grid,
    cot_grid,
    key_block,
    value_block,
    key_pos,
    query_pos,
    log_total,
    offsets,
    score_scale,
):
    grad_scores, weights_low = score_grads(
        query_grid,
        cot_grid,
        key_block,
        value_block,
        key_pos,
        query_pos,
        log_total,
        offsets,
        score_scale,
    )
    grad_query = jnp.einsum(
        "gqnk,kgd->ngqd", grad_scores, key_block, preferred_element_type=jnp.float32
    )
    grad_key = jnp.einsum(
        "gqnk,ngqd->kgd", grad_scores, query_grid, preferred_element_type=jnp.float32
    )
    grad_value = jnp.einsum(
        "gqnk,ngqd->kgd", weights_low, cot_grid, preferred_element_type=jnp.float32
    )
    return (grad_query, grad_key, grad_value)


def local(queries, rollout_keys, rollout_values, prompt_keys, prompt_values, grad_out, lengths):
    query_rows = queries[0]
    row_count, head_count, head_dim = query_rows.shape
    group_count = rollout_keys.shape[2]
    per_group = head_count // group_count
    query_grid = query_rows.reshape(row_count, group_count, per_group, head_dim)
    score_scale = head_dim ** (-0.5)
    first_row = lax.axis_index("seq") * row_count
    last_row = first_row + row_count - 1
    query_pos = first_row + jnp.arange(row_count, dtype=jnp.int32)
    seq_length = lengths[0]
    device_live = first_row < seq_length
    total_rows = row_count * lax.axis_size("seq")
    prompt_full_keys, prompt_full_values = (
        lax.all_gather(prompt_keys, ("seq", "roll"), axis=0, tiled=True),
        lax.all_gather(prompt_values, ("seq", "roll"), axis=0, tiled=True),
    )
    prompt_rows = prompt_full_keys.shape[0]
    span_rows = math.gcd(math.gcd(prompt_rows, total_rows), 512)
    prompt_pos = jnp.full((span_rows,), -1, jnp.int32)
    own_keys = rollout_keys[0]
    own_values = rollout_values[0]
    stat_shape = (group_count, per_group, row_count)
    maxima = jnp.full(stat_shape, -jnp.inf, jnp.float32)
    for counter in range(prompt_rows // span_rows):
        lower = counter * span_rows
        maxima = max_block(
            maxima,
            query_grid,
            prompt_full_keys[lower : lower + span_rows],
            prompt_pos,
            query_pos,
            score_scale,
        )

    def rollout_max(carried, key_block, block_start):
        key_pos = block_start + jnp.arange(key_block.shape[0], dtype=jnp.int32)
        return lax.cond(
            (block_start <= last_row) & device_live,
            lambda inner: max_block(inner, query_grid, key_block, key_pos, query_pos, score_scale),
            lambda inner: inner,
            carried,
        )

    gathered_keys, gathered_values = (
        lax.all_gather(own_keys, "seq", axis=0, tiled=True),
        lax.all_gather(own_values, "seq", axis=0, tiled=True),
    )

    def max_loop(counter, carried):
        block_start = counter * span_rows
        key_block = lax.dynamic_slice_in_dim(gathered_keys, block_start, span_rows, 0)
        return rollout_max(carried, key_block, block_start)

    maxima = lax.fori_loop(0, total_rows // span_rows, max_loop, maxima)
    running = (jnp.zeros(stat_shape, jnp.float32), jnp.zeros(stat_shape + (head_dim,), jnp.float32))
    for counter in range(prompt_rows // span_rows):
        lower = counter * span_rows
        running = forward_block(
            running,
            maxima,
            query_grid,
            prompt_full_keys[lower : lower + span_rows],
            prompt_full_values[lower : lower + span_rows],
            prompt_pos,
            query_pos,
            score_scale,
        )

    def forward_loop(counter, carried):
        block_start = counter * span_rows
        key_block = lax.dynamic_slice_in_dim(gathered_keys, block_start, span_rows, 0)
        value_block = lax.dynamic_slice_in_dim(gathered_values, block_start, span_rows, 0)
        key_pos = block_start + jnp.arange(span_rows, dtype=jnp.int32)
        return lax.cond(
            (block_start <= last_row) & device_live,
            lambda inner: forward_block(
                inner, maxima, query_grid, key_block, value_block, key_pos, query_pos, score_scale
            ),
            lambda inner: inner,
            carried,
        )

    running = lax.fori_loop(0, total_rows // span_rows, forward_loop, running)
    totals, summed = running
    normalized = summed / totals[..., None]
    row_valid = query_pos < seq_length
    flat_out = normalized.transpose(2, 0, 1, 3).reshape(row_count, head_count, head_dim)
    attention_rows = jnp.where(row_valid[:, None, None], flat_out, 0.0).astype(jnp.bfloat16)
    log_total = maxima + jnp.log(totals)
    cot_rows = jnp.where(row_valid[:, None, None], grad_out[0], jnp.zeros_like(grad_out[0]))
    cot_grid = cot_rows.reshape(row_count, group_count, per_group, head_dim)
    offsets = jnp.sum(cot_grid.transpose(1, 2, 0, 3).astype(jnp.float32) * normalized, -1)
    grad_query = jnp.zeros((row_count, group_count, per_group, head_dim), jnp.float32)
    prompt_key_parts = []
    prompt_value_parts = []
    for counter in range(prompt_rows // span_rows):
        lower = counter * span_rows
        block_grads = backward_block(
            query_grid,
            cot_grid,
            prompt_full_keys[lower : lower + span_rows],
            prompt_full_values[lower : lower + span_rows],
            prompt_pos,
            query_pos,
            log_total,
            offsets,
            score_scale,
        )
        grad_query = grad_query + block_grads[0]
        prompt_key_parts.append(block_grads[1])
        prompt_value_parts.append(block_grads[2])
    prompt_key_terms = jnp.concatenate(prompt_key_parts, axis=0)
    prompt_value_terms = jnp.concatenate(prompt_value_parts, axis=0)

    def backward_loop(counter, carried):
        block_start = counter * span_rows
        key_block = lax.dynamic_slice_in_dim(gathered_keys, block_start, span_rows, 0)
        value_block = lax.dynamic_slice_in_dim(gathered_values, block_start, span_rows, 0)
        key_pos = block_start + jnp.arange(span_rows, dtype=jnp.int32)

        def accumulate(carried_in):
            query_acc, key_acc, value_acc = carried_in
            block_grads = backward_block(
                query_grid,
                cot_grid,
                key_block,
                value_block,
                key_pos,
                query_pos,
                log_total,
                offsets,
                score_scale,
            )
            key_acc = lax.dynamic_update_slice_in_dim(key_acc, block_grads[1], block_start, 0)
            value_acc = lax.dynamic_update_slice_in_dim(value_acc, block_grads[2], block_start, 0)
            return (query_acc + block_grads[0], key_acc, value_acc)

        return lax.cond(
            (block_start <= last_row) & device_live,
            accumulate,
            lambda carried_in: carried_in,
            carried,
        )

    zero_keys = jnp.zeros((total_rows, group_count, head_dim), jnp.float32)
    grad_query, key_grads, value_grads = lax.fori_loop(
        0, total_rows // span_rows, backward_loop, (grad_query, zero_keys, zero_keys)
    )
    rollout_key_sum, rollout_value_sum = (
        lax.psum_scatter(key_grads, "seq", scatter_dimension=0, tiled=True),
        lax.psum_scatter(value_grads, "seq", scatter_dimension=0, tiled=True),
    )
    prompt_key_sum, prompt_value_sum = (
        lax.psum_scatter(prompt_key_terms, ("seq", "roll"), scatter_dimension=0, tiled=True),
        lax.psum_scatter(prompt_value_terms, ("seq", "roll"), scatter_dimension=0, tiled=True),
    )
    grad_rows = grad_query.reshape(row_count, head_count, head_dim).astype(jnp.bfloat16)
    return (
        attention_rows[None],
        grad_rows[None],
        rollout_key_sum.astype(jnp.bfloat16)[None],
        rollout_value_sum.astype(jnp.bfloat16)[None],
        prompt_key_sum.astype(jnp.bfloat16),
        prompt_value_sum.astype(jnp.bfloat16),
    )


def solution(mesh):
    placed = (
        P("roll", "seq", "head", None),
        P("roll", "seq", "head", None),
        P("roll", "seq", "head", None),
        P(("seq", "roll"), "head", None),
        P(("seq", "roll"), "head", None),
        P("roll", "seq", "head", None),
        P("roll"),
    )
    return jax.shard_map(
        local,
        mesh=mesh,
        in_specs=placed,
        out_specs=(
            P("roll", "seq", "head", None),
            P("roll", "seq", "head", None),
            P("roll", "seq", "head", None),
            P("roll", "seq", "head", None),
            P(("seq", "roll"), "head", None),
            P(("seq", "roll"), "head", None),
        ),
        check_vma=False,
    )
```

profile of v0, /device:TPU:0, one launch (start us, length us, event | category | flops | bytes accessed | tf_op | source)
XLA Modules:
  0.0 723.2 jit_solution(3325765659971104703)
XLA Ops:
  12.5 86.2 %all_gather.12 = bf16[1024,2,128]{2,0,1:T(8,128)(2,1)S(1)} all-gather(bf16[32,2,128]{2,0,1:T(8,128)(2,1)S(1)} %copy.29), channel_id=1, replica_groups=mesh['seq'=16,'roll'=2,'head'=4] {'seq','roll'}, dimensions={0}, use_global_device_ids=true | all-gather | bytes 540672 | tf_op jit(solution)/shard_map/all_gather | solution.py:107
  106.0 4.5 bitcast_reduce_fusion
  111.8 78.5 %all_gather.14 = bf16[1024,2,128]{2,0,1:T(8,128)(2,1)S(1)} all-gather(bf16[32,2,128]{2,0,1:T(8,128)(2,1)S(1)} %copy.32), channel_id=1, replica_groups=mesh['seq'=16,'roll'=2,'head'=4] {'seq','roll'}, dimensions={0}, use_global_device_ids=true | all-gather | bytes 540672 | tf_op jit(solution)/shard_map/all_gather | solution.py:108
  190.3 2.6 while.51
  193.0 6.4 fusion.75
  201.3 2.7 fusion.96
  204.0 6.3 while.52
  204.0 5.9 conditional.10
  204.2 3.0 fusion.13
  207.2 2.7 fusion.20
  210.3 2.9 fusion.94
  213.2 14.7 %fusion.102 = f32[512,2,128]{0,2,1:T(8,128)S(1)} fusion(bf16[192,2,8,128]{3,0,2,1:T(8,128)(2,1)S(1)} %get-tuple-element.1320, f32[2,512,192,8]{1,2,3,0:T(8,128)} %get-tuple-element.1041, f32[2,8,192]{2,1,0:T(8,128)S(1)} %log_add_fusion, pred[192]{0:T(512)(128)(4,1)S(1)} %fusion.111), kind=kOutput, calls=%fused_computation.113 | convolution fusion | flops 408944640 | bytes 7614656 | tf_op jit(solution)/shard_map/gqnk,ngqd->kgd/dot_general | solution.py:87
  229.7 3.6 fusion.62
  233.3 2.4 fusion.65
  240.6 200.7 %all-reduce.6 = bf16[1024,2,128]{2,1,0:T(2,128)(2,1)} all-reduce(f32[1024,2,128]{2,1,0:T(2,128)} %copy.43), channel_id=7, replica_groups=mesh['seq'=16,'roll'=2,'head'=4] {'seq','roll'}, use_global_device_ids=true, to_apply=%region_22.23.clone | all-reduce | flops 262144 | bytes 1572864
  441.3 4.2 convolution_bitcast_fusion.1
  451.7 13.6 %while.53 = (s32[]{:T(128)}, f32[192,2,8,128]{3,0,2,1:T(8,128)S(1)}, f32[3072,2,128]{2,0,1:T(8,128)}, f32[3072,2,128]{2,0,1:T(8,128)}, s32[]{:T(128)}, /*index=5...) while((s32[]{:T(128)}, ...), condition=%wide.region_18.19_spmd.clone, body=%wide.region_15.18_spmd.clone.sunk | while | flops 2031059712 | bytes 39927200 | solution.py:239
  451.7 13.3 %conditional.11 = ((f32[192,2,8,128]{3,0,2,1:T(8,128)S(1)}, f32[3072,2,128]{2,0,1:T(8,128)}, f32[3072,2,128]{2,0,1:T(8,128)})) conditional(s32[]{:T(128)} %convert_element_type.158, (f32[192,2,8,128]{3,0,2,1:T(8,128)S(1)}, f32[3072,2,128]{2,0,1:T(8,128)}, f32[3072,2,128]{2,0,1:T(8,128)}) %tuple.156, (s32[]{:T(128)}, s32[512]{0:T(512)S(1)}, ...), branch_computations={%region_16.16_spmd, %region_17.17_spmd} | conditional | flops 2031059712 | bytes 39924088 | solution.py:231
  453.9 3.5 fusion.34
  461.5 3.5 fusion.45
  465.3 7.3 %copy.41 = f32[3072,2,128]{2,1,0:T(2,128)} copy(f32[3072,2,128]{2,0,1:T(8,128)} %get-tuple-element.874) | data formatting | bytes 6291456 | tf_op jit(solution)/shard_map/while | solution.py:239
  472.5 12.4 %copy.42 = f32[3072,2,128]{2,1,0:T(2,128)} copy(f32[3072,2,128]{2,0,1:T(8,128)S(1)} %copy-done.3) | data formatting | bytes 6291456 | tf_op jit(solution)/shard_map/while | solution.py:239
  488.9 183.9 %all-reduce.7 = (bf16[3072,2,128]{2,1,0:T(2,128)(2,1)S(1)}, bf16[3072,2,128]{2,1,0:T(2,128)(2,1)}) all-reduce(f32[3072,2,128]{2,1,0:T(2,128)} %copy.41, f32[3072,2,128]{2,1,0:T(2,128)} %copy.42), channel_id=4, replica_groups=mesh['seq'=16,'roll'=2,'head'=4] {'seq'}, use_global_device_ids=true, to_apply=%region_19.20.clone | all-reduce | flops 1572864 | bytes 9437184
  677.9 37.2 %reduce-scatter.2.cloned.1.call-done = f32[32,2,128]{2,0,1:T(8,128)} async-done(((f32[1024,2,128]{2,0,1:T(8,128)}), f32[32,2,128]{2,0,1:T(8,128)}) %reduce-scatter.2.cloned.1.call-update) | async-done | bytes 32784 | tf_op jit(solution)/shard_map/reduce_scatter | solution.py:247
  (142 shorter events, 48.0 us)
Async XLA Ops:
  7.2 183.2 %all-gather.5.cloned.1.call-start = ((), (), s32[]{:S(2)}) async-start(), calls=%async_computation.2 | async-start | bytes 1671168 | tf_op jit(solution)/shard_map/all_gather | solution.py:138
  8.8 195.2 %all-gather.7.cloned.1.call-start = ((), (), s32[]{:S(2)}) async-start(), calls=%async_computation.3 | async-start | bytes 1671168 | tf_op jit(solution)/shard_map/all_gather | solution.py:139
  10.4 704.6 %reduce-scatter.2.cloned.1.call-start = ((), (), s32[]{:S(2)}) async-start(), calls=%async_computation.1 | async-start | bytes 1081344 | tf_op jit(solution)/shard_map/reduce_scatter | solution.py:247
  105.9 4.5 copy-start
  190.3 9.1 %copy-start.8 = (bf16[1024,2,128]{2,0,1:T(8,128)(2,1)}, bf16[1024,2,128]{2,0,1:T(8,128)(2,1)S(1)}, u32[]{:S(2)}) copy-start(bf16[1024,2,128]{2,0,1:T(8,128)(2,1)S(1)} %all_gather.14) | copy-start | bytes 1572868
  192.9 8.3 %slice-start = ((s8[6291456]{0:T(1024)(128)(4,1)}), s8[4194304]{0:T(1024)(128)(4,1)S(1)}, s32[]{:S(2)}) async-start(s8[6291456]{0:T(1024)(128)(4,1)} %bitcast.240), calls=%async_computation.4 | async-start | bytes 8388608
  193.0 6.6 copy-start.1
  193.0 8.3 %slice-start.1 = ((s8[6291456]{0:T(1024)(128)(4,1)}), s8[2097152]{0:T(1024)(128)(4,1)S(1)}, s32[]{:S(2)}) async-start(s8[6291456]{0:T(1024)(128)(4,1)} %bitcast.240), calls=%async_computation.5 | async-start | bytes 4194304
  210.3 19.3 %copy-start.4 = (f32[2,8,192,128]{3,2,1,0:T(8,128)}, f32[2,8,192,128]{3,2,1,0:T(8,128)S(1)}, u32[]{:S(2)}) copy-start(f32[2,8,192,128]{3,2,1,0:T(8,128)S(1)} %get-tuple-element.871) | copy-start | bytes 4718596
  210.3 17.6 %slice-start.2 = ((s8[6291456]{0:T(1024)(128)(4,1)}), s8[4194304]{0:T(1024)(128)(4,1)S(1)}, s32[]{:S(2)}) async-start(s8[6291456]{0:T(1024)(128)(4,1)} %bitcast.242), calls=%async_computation.6 | async-start | bytes 8388608
  213.2 20.1 %copy-start.6 = (bf16[192,2,8,128]{3,0,2,1:T(8,128)(2,1)}, bf16[192,2,8,128]{3,0,2,1:T(8,128)(2,1)S(1)}, u32[]{:S(2)}) copy-start(bf16[192,2,8,128]{3,0,2,1:T(8,128)(2,1)S(1)} %get-tuple-element.1320) | copy-start | bytes 2359300
  213.2 14.7 %slice-start.3 = ((s8[6291456]{0:T(1024)(128)(4,1)}), s8[2097152]{0:T(1024)(128)(4,1)S(1)}, s32[]{:S(2)}) async-start(s8[6291456]{0:T(1024)(128)(4,1)} %bitcast.242), calls=%async_computation.7 | async-start | bytes 4194304
  213.2 16.4 %slice-start.4 = ((s8[6291456]{0:T(1024)(128)(4,1)}), s8[4194304]{0:T(1024)(128)(4,1)S(1)}, s32[]{:S(2)}) async-start(s8[6291456]{0:T(1024)(128)(4,1)} %bitcast.244), calls=%async_computation.8 | async-start | bytes 8388608
  228.0 1.7 slice-start.5
  228.0 1.7 copy-start.9
  441.3 4.2 copy-start.2
  451.7 2.2 copy-start.7
  465.3 7.3 %copy-start.3 = (f32[3072,2,128]{2,0,1:T(8,128)S(1)}, f32[3072,2,128]{2,0,1:T(8,128)}, u32[]{:S(2)}) copy-start(f32[3072,2,128]{2,0,1:T(8,128)} %get-tuple-element.875) | copy-start | bytes 9437188
  465.3 19.6 %copy-start.5 = (f32[512,2,128]{2,0,1:T(8,128)S(1)}, f32[512,2,128]{2,0,1:T(8,128)}, u32[]{:S(2)}) copy-start(f32[512,2,128]{2,0,1:T(8,128)} %convolution_bitcast_fusion.1) | copy-start | bytes 1572868
Sparse Core Ops, SparseCore 0:
  10.7 46.6 all-gather.4
  60.1 43.4 all-gather.6
  486.2 228.8 reduce-scatter.1
where the time goes:
time: 728 us; the launch traced here: 723 us
  blocking collectives  549 us (75%)
  matrix products  63.1 us (9%)
  local copies, waits for them, and re-layouts  40.8 us (6%)
  waiting for transfers between devices  37.3 us (5%)
  between operations  16.3 us (2%)
  other arithmetic  15.2 us (2%)
    unnamed x2, blocking collectives  385 us
    all_gather x1, blocking collectives, local(): lax.all_gather(prompt_keys, ('seq', 'roll'), axis=0, tiled=True)  86.2 us
    all_gather x1, blocking collectives, local(): lax.all_gather(prompt_values, ('seq', 'roll'), axis=0, tiled=True)  78.5 us
    reduce_scatter x1, waiting for transfers between devices, local(): lax.psum_scatter(prompt_key_terms, ('seq', 'roll'), scatter_dimension=0,...  37.2 us
    dot_general x3, matrix products, backward_block(): jnp.einsum('gqnk,ngqd->kgd', weights_low, cot_grid, preferred_element_typ...  19.8 us
    while x2, local copies, waits for them, and re-layouts, local(): lax.fori_loop(0, total_rows // span_rows, backward_loop, (grad_query, zer...  19.6 us
  transfers between devices with their start and end apart: 3, of which 1 were waited for; matrix products, arithmetic and copies ran while one was open for 5% of the time, Pallas kernels for 0%

commit v1 on v0

v1 whole, which is shorter than its diff:
```python
import math

import jax
import jax.numpy as jnp
from jax import lax
from jax.experimental import pallas as pl
from jax.experimental.pallas import tpu as pltpu
from jax.sharding import PartitionSpec as P

f32, bf16 = jnp.float32, jnp.bfloat16
N = 16
BLK = 192
PRM = 1024
PB = 64
HD = 128
PG = 8
RB = BLK * PG
TILE = 4 * BLK
HALF = 2 * BLK
RC = RB // 2
SCALE = HD**-0.5
SCALE2 = SCALE * math.log2(math.e)
NEG = -1e30
MESH = pl.DeviceIdType.MESH

NN = (((1,), (0,)), ((), ()))
NT = (((1,), (1,)), ((), ()))
TN = (((0,), (0,)), ((), ()))


def dot(a, b, dims=NN):
    return lax.dot_general(a, b, dims, preferred_element_type=f32)


def kernel(
    q_in, do_in, kv_in, pk_in,
    out, dq, dkv_out, dp_out,
    q2, do2, kv, p64, acc, mx, tot, lse, off, o16, dk, dv, g16, recv, recvp, psum, prem,
    lsem, psem, kvs, kvr, pps, ppr, qsem, osem, gs, gr, gps, gpr, fsem,
):
    s = lax.axis_index("seq")
    r = lax.axis_index("roll")
    hs = s // 8
    partner = N - 1 - s
    high = jnp.maximum(s, partner)
    need = (high // 2) * 2 + 1

    barrier = pltpu.get_barrier_semaphore()
    for d in range(1, N):
        pl.semaphore_signal(barrier, inc=1, device_id={"seq": (s + d) % N}, device_id_type=MESH)
    pl.semaphore_signal(barrier, inc=1, device_id={"roll": 1 - r}, device_id_type=MESH)
    pl.semaphore_wait(barrier, N)

    def remote(src, dst, ssem, rsem, **where):
        return pltpu.make_async_remote_copy(
            src_ref=src, dst_ref=dst, send_sem=ssem, recv_sem=rsem,
            device_id=where, device_id_type=MESH,
        )

    rows32 = pl.ds(pl.multiple_of(r * 32, 32), 32)
    p_out = remote(pk_in, p64.at[:, :, rows32, :], psem.at[0], psem.at[1], roll=1 - r)
    p_out.start()
    p_own = pltpu.make_async_copy(pk_in, p64.at[:, :, rows32, :], psem.at[2])
    p_own.start()
    own_q = pltpu.make_async_copy(q_in.at[hs], q2.at[0], lsem.at[0])
    own_q.start()
    own_do = pltpu.make_async_copy(do_in.at[hs], do2.at[0], lsem.at[1])
    own_do.start()

    def kv_rows(j):
        return kv.at[:, pl.ds(pl.multiple_of(PRM + j * BLK, 64), BLK), :]

    def kv_copy(t):
        return remote(kv_in.at[t // 8], kv_rows(s), kvs.at[t], kvr.at[s], seq=t)

    def kv_wanted(t):
        return s <= (jnp.maximum(t, N - 1 - t) // 2) * 2 + 1

    own_kv = pltpu.make_async_copy(kv_in.at[hs], kv_rows(s), lsem.at[2])
    own_kv.start()

    def p_rows(j):
        return kv.at[:, pl.ds(pl.multiple_of(j * PB, PB), PB), :]

    def p_copy(t):
        return remote(p64.at[t // 8], p_rows(s), pps.at[t], ppr.at[s], seq=t)

    p_own.wait()
    p_out.wait_recv()
    own_p = pltpu.make_async_copy(p64.at[hs], p_rows(s), lsem.at[3])
    own_p.start()

    @pl.loop(1, N)
    def _(d):
        p_copy((s + d) % N).start()

    q_out = remote(q_in.at[1 - hs], q2.at[1], qsem.at[0], qsem.at[1], seq=partner)
    q_out.start()

    @pl.loop(1, N)
    def _(d):
        t = (s + d) % N

        @pl.when(kv_wanted(t))
        def _():
            kv_copy(t).start()

    do_out = remote(do_in.at[1 - hs], do2.at[1], qsem.at[2], qsem.at[3], seq=partner)
    do_out.start()

    def block_of(b):
        return jnp.where(b == 0, s, partner)

    def masked_scores(scores, k0, q0):
        key_pos = k0 - PRM + lax.broadcasted_iota(jnp.int32, scores.shape, 0)
        query_pos = q0 + lax.broadcasted_iota(jnp.int32, scores.shape, 1) // PG
        return jnp.where(key_pos <= query_pos, scores, NEG)

    def forward_tile(b, k0, size, masked):
        rows = pl.ds(pl.multiple_of(k0, 64), size)
        scores = dot(kv[0, rows, :], q2[b], NT) * SCALE2
        if masked:
            scores = masked_scores(scores, k0, block_of(b) * BLK)
        old = mx[b]
        new = jnp.maximum(old, jnp.max(scores, 0, keepdims=True))
        lifted = jnp.exp2(scores - new)
        shrink = jnp.exp2(old - new)
        mx[b] = new
        tot[b] = tot[b] * shrink + jnp.sum(lifted, 0, keepdims=True)
        acc[b] = acc[b] * shrink + dot(kv[1, rows, :], lifted.astype(bf16), TN)

    acc[...] = jnp.zeros_like(acc)
    mx[...] = jnp.full_like(mx, NEG)
    tot[...] = jnp.zeros_like(tot)
    own_q.wait()
    own_p.wait()

    @pl.loop(1, N)
    def _(d):
        t = (s + d) % N
        remote(p64.at[hs], p_rows(t), pps.at[t], ppr.at[t], seq=t).wait_recv()

    @pl.loop(0, 2)
    def _(b):
        @pl.when(b == 1)
        def _():
            q_out.wait_recv()

        forward_tile(b, 0, PRM, False)

    def wait_tile(tile):
        @pl.loop(0, 4)
        def _(i):
            j = tile * 4 + i

            @pl.when(j == s)
            def _():
                own_kv.wait()

            @pl.when((j != s) & (j <= need))
            def _():
                remote(kv_in.at[hs], kv_rows(j), kvs.at[j], kvr.at[j], seq=j).wait_recv()

    @pl.loop(0, 2)
    def _(b):
        blk = block_of(b)
        last = blk // 4

        @pl.loop(0, last)
        def _(tile):
            @pl.when((b == 0) | (tile > s // 4))
            def _():
                wait_tile(tile)

            forward_tile(b, PRM + tile * TILE, TILE, False)

        @pl.when((b == 0) | (last > s // 4))
        def _():
            wait_tile(last)

        @pl.loop(0, 1 + (blk % 4) // 2)
        def _(half):
            forward_tile(b, PRM + last * TILE + half * HALF, HALF, True)

    own_do.wait()
    do_out.wait_recv()

    @pl.loop(0, 2)
    def _(b):
        total = tot[b]
        normal = acc[b] / total
        lse[b] = mx[b] + jnp.log2(total)
        off[b] = jnp.sum(normal * do2[b].astype(f32).T, 0, keepdims=True)
        o16[b] = normal.T.astype(bf16)

    own_out = pltpu.make_async_copy(o16.at[0], out.at[hs], lsem.at[4])
    own_out.start()
    out_out = remote(o16.at[1], out.at[hs], osem.at[0], osem.at[1], seq=partner)
    out_out.start()

    acc[...] = jnp.zeros_like(acc)
    dk[...] = jnp.zeros_like(dk)
    dv[...] = jnp.zeros_like(dv)

    def backward_tile(b, k0, size, masked):
        rows = pl.ds(pl.multiple_of(k0, 64), size)

        for c in range(RB // RC):
            part = pl.ds(c * RC, RC)
            keys, values = kv[0, rows, :], kv[1, rows, :]
            queries, cot = q2[b, part, :], do2[b, part, :]
            scores = dot(keys, queries, NT) * SCALE2
            if masked:
                scores = masked_scores(scores, k0, block_of(b) * BLK + c * (RC // PG))
            weights = jnp.exp2(scores - lse[b, :, part])
            grads = (weights * (dot(values, cot, NT) - off[b, :, part])).astype(bf16)
            dv[rows, :] += dot(weights.astype(bf16), cot)
            dk[rows, :] += dot(grads, queries)
            acc[b, :, part] += dot(keys, grads, TN)

    def finish_rows(k0, size):
        rows = pl.ds(pl.multiple_of(k0, 64), size)
        g16[0, rows, :] = (dk[rows, :] * SCALE).astype(bf16)
        g16[1, rows, :] = dv[rows, :].astype(bf16)

    def grad_rows(j):
        return g16.at[:, pl.ds(pl.multiple_of(PRM + j * BLK, 64), BLK), :]

    def grad_copy(j):
        return remote(grad_rows(j), recv.at[s], gs.at[j], gr.at[s], seq=j)

    own_g = pltpu.make_async_copy(grad_rows(s), recv.at[s], lsem.at[5])

    def send_tile(tile):
        finish_rows(PRM + tile * TILE, TILE)

        @pl.loop(0, 4)
        def _(i):
            j = tile * 4 + i

            @pl.when(j == s)
            def _():
                own_g.start()

            @pl.when((j != s) & (j <= high))
            def _():
                grad_copy(j).start()

    def gp_rows(t):
        return g16.at[:, pl.ds(pl.multiple_of(t * PB, PB), PB), :]

    def gp_copy(t):
        return remote(gp_rows(t), recvp.at[s], gps.at[t], gpr.at[s], seq=t)

    own_gp = pltpu.make_async_copy(gp_rows(s), recvp.at[s], lsem.at[6])
    dq_out = remote(o16.at[3], dq.at[hs], osem.at[2], osem.at[3], seq=partner)

    @pl.loop(0, 2)
    def _(i):
        b = 1 - i
        blk = block_of(b)
        last = blk // 4
        backward_tile(b, 0, PRM, False)

        @pl.when(b == 0)
        def _():
            finish_rows(0, PRM)
            own_gp.start()

            @pl.loop(1, N)
            def _(d):
                gp_copy((s + d) % N).start()

        @pl.loop(0, last)
        def _(tile):
            backward_tile(b, PRM + tile * TILE, TILE, False)

            @pl.when(b == 0)
            def _():
                send_tile(tile)

        @pl.loop(0, 1 + (blk % 4) // 2)
        def _(half):
            backward_tile(b, PRM + last * TILE + half * HALF, HALF, True)

        o16[2 + b] = (acc[b] * SCALE).T.astype(bf16)

        @pl.when(b == 0)
        def _():
            send_tile(last)

        @pl.when(b == 1)
        def _():
            dq_out.start()

            @pl.loop(s // 4 + 1, partner // 4 + 1)
            def _(tile):
                send_tile(tile)

    own_dq = pltpu.make_async_copy(o16.at[2], dq.at[hs], lsem.at[7])
    own_dq.start()

    own_gp.wait()

    @pl.loop(1, N)
    def _(d):
        t = (s + d) % N
        remote(gp_rows(t), recvp.at[t], gps.at[t], gpr.at[t], seq=t).wait_recv()

    for h in range(2):
        total = recvp[8 * h].astype(f32)
        for i in range(1, 8):
            total = total + recvp[8 * h + i].astype(f32)
        psum[h] = total
    theirs = pl.ds(pl.multiple_of((1 - r) * 32, 32), 32)
    f_out = remote(psum.at[:, :, theirs, :], prem, fsem.at[0], fsem.at[1], roll=1 - r)
    f_out.start()

    own_g.wait()

    @pl.loop(1, N)
    def _(d):
        t = (s + d) % N

        @pl.when(s <= jnp.maximum(t, N - 1 - t))
        def _():
            remote(grad_rows(s), recv.at[t], gs.at[t], gr.at[t], seq=t).wait_recv()

    total0 = jnp.zeros(recv.shape[1:], f32)
    total1 = jnp.zeros(recv.shape[1:], f32)
    for i in range(8):
        total0 = total0 + jnp.where(s <= N - 1 - i, recv[i].astype(f32), 0.0)
        total1 = total1 + jnp.where(s <= 8 + i, recv[8 + i].astype(f32), 0.0)
    dkv_out[0] = total0.astype(bf16)
    dkv_out[1] = total1.astype(bf16)
    f_out.wait_recv()
    dp_out[...] = (psum[:, :, rows32, :] + prem[...]).astype(bf16)

    p_out.wait_send()
    q_out.wait_send()
    do_out.wait_send()
    out_out.wait()
    dq_out.wait()
    f_out.wait_send()
    own_out.wait()
    own_dq.wait()

    @pl.loop(1, N)
    def _(d):
        t = (s + d) % N
        p_copy(t).wait_send()
        gp_copy(t).wait_send()

        @pl.when(kv_wanted(t))
        def _():
            kv_copy(t).wait_send()

        @pl.when(t <= high)
        def _():
            grad_copy(t).wait_send()


def attention(q_rows, do_rows, kv_rows, prompt_rows):
    any_spec = pl.BlockSpec(memory_space=pl.ANY)
    vmem = pl.BlockSpec(memory_space=pltpu.VMEM)
    dma = pltpu.SemaphoreType.DMA
    return pl.pallas_call(
        kernel,
        out_shape=[
            jax.ShapeDtypeStruct((2, RB, HD), bf16),
            jax.ShapeDtypeStruct((2, RB, HD), bf16),
            jax.ShapeDtypeStruct((2, 2, BLK, HD), bf16),
            jax.ShapeDtypeStruct((2, 2, 32, HD), bf16),
        ],
        in_specs=[any_spec] * 4,
        out_specs=[any_spec, any_spec, vmem, vmem],
        scratch_shapes=[
            pltpu.VMEM((2, RB, HD), bf16),
            pltpu.VMEM((2, RB, HD), bf16),
            pltpu.VMEM((2, PRM + N * BLK, HD), bf16),
            pltpu.VMEM((2, 2, PB, HD), bf16),
            pltpu.VMEM((2, HD, RB), f32),
            pltpu.VMEM((2, 1, RB), f32),
            pltpu.VMEM((2, 1, RB), f32),
            pltpu.VMEM((2, 1, RB), f32),
            pltpu.VMEM((2, 1, RB), f32),
            pltpu.VMEM((4, RB, HD), bf16),
            pltpu.VMEM((PRM + N * BLK, HD), f32),
            pltpu.VMEM((PRM + N * BLK, HD), f32),
            pltpu.VMEM((2, PRM + N * BLK, HD), bf16),
            pltpu.VMEM((N, 2, BLK, HD), bf16),
            pltpu.VMEM((N, 2, PB, HD), bf16),
            pltpu.VMEM((2, 2, PB, HD), f32),
            pltpu.VMEM((2, 2, 32, HD), f32),
            dma((8,)),
            dma((3,)),
            dma((N,)),
            dma((N,)),
            dma((N,)),
            dma((N,)),
            dma((4,)),
            dma((4,)),
            dma((N,)),
            dma((N,)),
            dma((N,)),
            dma((N,)),
            dma((2,)),
        ],
        compiler_params=pltpu.CompilerParams(
            collective_id=0, has_side_effects=True, vmem_limit_bytes=58 * 2**20
        ),
    )(q_rows, do_rows, kv_rows, prompt_rows)


def local(queries, rollout_keys, rollout_values, prompt_keys, prompt_values, grad_out, lengths):
    first_row = lax.axis_index("seq") * BLK
    valid = ((first_row + jnp.arange(BLK, dtype=jnp.int32)) < lengths[0])[None, :, None, None]

    def by_group(rows):
        return rows.reshape(BLK, 2, PG, HD).transpose(1, 0, 2, 3)

    def merged(rows):
        return rows.transpose(1, 0, 2, 3).reshape(1, BLK, 2 * PG, HD)

    q_rows = by_group(queries[0]).reshape(2, RB, HD)
    cot = by_group(grad_out[0])
    do_rows = jnp.where(valid, cot, jnp.zeros_like(cot)).reshape(2, RB, HD)
    kv_rows = jnp.stack([rollout_keys[0], rollout_values[0]]).transpose(2, 0, 1, 3)
    prompt_rows = jnp.stack([prompt_keys, prompt_values]).transpose(2, 0, 1, 3)
    out, dq, dkv, dprompt = attention(q_rows, do_rows, kv_rows, prompt_rows)
    out = out.reshape(2, BLK, PG, HD)
    out = jnp.where(valid, out, jnp.zeros_like(out))
    dkv = dkv.transpose(1, 2, 0, 3)
    dprompt = dprompt.transpose(1, 2, 0, 3)
    return (
        merged(out),
        merged(dq.reshape(2, BLK, PG, HD)),
        dkv[0][None],
        dkv[1][None],
        dprompt[0],
        dprompt[1],
    )


def solution(mesh):
    rows = P("roll", "seq", "head", None)
    prompt = P(("seq", "roll"), "head", None)
    return jax.shard_map(
        local,
        mesh=mesh,
        in_specs=(rows, rows, rows, prompt, prompt, rows, P("roll")),
        out_specs=(rows, rows, rows, rows, prompt, prompt),
        check_vma=False,
    )
```

time: 728 us -> 119 us (0.16)
  blocking collectives: 549 us -> 0 us
  Pallas kernels: 0 us -> 104 us
  matrix products: 63.1 us -> 0 us
  waiting for transfers between devices: 37.3 us -> 0 us
  local copies, waits for them, and re-layouts: 40.8 us -> 6.34 us
  between operations: 16.3 us -> 1.47 us
  other arithmetic: 15.2 us -> 5.17 us
    unnamed x2 -> x0, blocking collectives: 385 us -> none
    all_gather x2 -> x0, blocking collectives: 165 us -> none  [the longest x1 86.2 us: local(): lax.all_gather(prompt_keys, ('seq', 'roll'), axis=0, tiled=True)]
    pallas_call x0 -> x1, Pallas kernels: none -> 104 us  [attention(): pl.pallas_call(kernel, out_shape=[jax.ShapeDtypeStruct((2, RB, HD), bf16)...]
    dot_general x20 -> x0, matrix products: 63.1 us -> none  [the longest x3 19.8 us: backward_block(): jnp.einsum('gqnk,ngqd->kgd', weights_low, cot_grid, preferred_element_typ...]
    reduce_scatter x1 -> x0, waiting for transfers between devices: 37.2 us -> none  [local(): lax.psum_scatter(prompt_key_terms, ('seq', 'roll'), scatter_dimension=0,...]
    while x2 -> x0, local copies, waits for them, and re-layouts: 19.6 us -> none  [local(): lax.fori_loop(0, total_rows // span_rows, backward_loop, (grad_query, zer...]
    reduce_sum x2 -> x0, other arithmetic: 9.33 us -> none  [the longest x1 6.45 us: forward_block(): totals = totals + jnp.sum(lifted, -1)]
  transfers between devices with their start and end apart: 3 -> 0, of which waited for: 1 -> 0; matrix products, arithmetic and copies ran while one was open for 5% -> 0% of each run, Pallas kernels for 0% -> 0%
where the time goes in v1:
time: 119 us; the launch traced here: 117 us
  Pallas kernels  104 us (87%)
  local copies, waits for them, and re-layouts  6.34 us (5%)
  other arithmetic  5.17 us (4%)
  between operations  1.47 us (1%)
    pallas_call x1, Pallas kernels, attention(): pl.pallas_call(kernel, out_shape=[jax.ShapeDtypeStruct((2, RB, HD), bf16)...  104 us
    unnamed x16, local copies, waits for them, and re-layouts  4.56 us

profile of v1, /device:TPU:0, one launch (start us, length us, event | category | flops | bytes accessed | tf_op | source)
XLA Modules:
  0.0 117.1 jit_solution(2649288230652899573)
XLA Ops:
  0.6 0.0 copy-start
  0.6 0.0 copy-start.2
  1.4 0.7 copy_bitcast_fusion.3
  2.2 0.6 maximum_bitcast_fusion.1.pk_in
  2.8 0.9 copy.15
  3.7 0.9 copy.16
  4.6 0.7 maximum_bitcast_fusion.kv_in
  5.3 0.0 copy-done
  5.3 0.0 copy-done.2
  5.3 1.5 %fusion.1 = (bf16[2,1536,128]{2,1,0:T(8,128)(2,1)}, bf16[2,1536,128]{2,1,0:T(8,128)(2,1)}) fusion(pred[192]{0:T(512)(128)(4,1)S(1)} %add_compare_fusion, bf16[1,192,16,128]{3,2,1,0:T(8,128)(2,1)S(1)} %copy-done, bf16[1,192,16,128]{3,2,1,0:T(8,128)(2,1)S(1)} %copy-done.2), kind=kLoop, calls=%fused_computation.5 | loop fusion | flops 393216 | bytes 3145920 | tf_op jit(solution)/shard_map/reshape | solution.py:427
  6.8 104.1 %shard_map.118 = (bf16[2,1536,128]{2,1,0:T(8,128)(2,1)}, bf16[2,1536,128]{2,1,0:T(8,128)(2,1)}, bf16[2,2,192,128]{3,2,1,0:T(8,128)(2,1)}, bf16[2,2,32,128]{3,2,1,0:T(8,128)(2,1)}) custom-call(bf16[2,1536,128]{2,1,0:T(8,128)(2,1)} %get-tuple-element.27.q_in, bf16[2,1536,128]{2,1,0:T(8,128)(2,1)} %get-tuple-element.26.do_in, ...), custom_call_target="tpu_custom_call" | custom-call | tf_op jit(solution)/shard_map/pallas_call | solution.py:367
  111.0 0.0 copy-start.4
  111.0 0.0 copy-start.3
  111.0 2.3 %copy_bitcast_fusion.1 = bf16[1,192,16,128]{3,2,1,0:T(8,128)(2,1)} fusion(bf16[2,1536,128]{2,1,0:T(8,128)(2,1)} %get-tuple-element.10, pred[192]{0:T(512)(128)(4,1)S(1)} %add_compare_fusion), kind=kLoop, calls=%fused_computation.3 | loop fusion | flops 393216 | bytes 1573056 | tf_op jit(solution)/shard_map/reshape | solution.py:423
  113.3 0.0 copy-done.4
  113.3 0.0 copy-start.1
  113.4 0.6 copy.24
  114.0 0.6 copy.23
  114.6 0.0 copy-done.3
  114.6 0.7 copy.22
  115.4 0.7 copy.21
  116.1 0.0 copy-done.1
  116.1 1.0 copy_bitcast_fusion
  (3 shorter events, 0.0 us)
Async XLA Ops:
  0.6 4.7 %copy-start = (bf16[1,192,16,128]{3,2,1,0:T(8,128)(2,1)S(1)}, bf16[1,192,16,128]{3,2,1,0:T(8,128)(2,1)}, u32[]{:S(2)}) copy-start(bf16[1,192,16,128]{3,2,1,0:T(8,128)(2,1)} %param.7) | copy-start | bytes 2359300
  0.6 4.7 %copy-start.2 = (bf16[1,192,16,128]{3,2,1,0:T(8,128)(2,1)S(1)}, bf16[1,192,16,128]{3,2,1,0:T(8,128)(2,1)}, u32[]{:S(2)}) copy-start(bf16[1,192,16,128]{3,2,1,0:T(8,128)(2,1)} %param.12) | copy-start | bytes 2359300
  111.0 2.3 %copy-start.4 = (bf16[2,2,32,128]{3,2,1,0:T(8,128)(2,1)S(1)}, bf16[2,2,32,128]{3,2,1,0:T(8,128)(2,1)}, u32[]{:S(2)}) copy-start(bf16[2,2,32,128]{3,2,1,0:T(8,128)(2,1)} %get-tuple-element.13) | copy-start | bytes 98308
  111.0 3.6 %copy-start.3 = (bf16[2,2,192,128]{3,2,1,0:T(8,128)(2,1)S(1)}, bf16[2,2,192,128]{3,2,1,0:T(8,128)(2,1)}, u32[]{:S(2)}) copy-start(bf16[2,2,192,128]{3,2,1,0:T(8,128)(2,1)} %get-tuple-element.12) | copy-start | bytes 589828
  113.3 2.8 %copy-start.1 = (bf16[2,1536,128]{2,1,0:T(8,128)(2,1)S(1)}, bf16[2,1536,128]{2,1,0:T(8,128)(2,1)}, u32[]{:S(2)}) copy-start(bf16[2,1536,128]{2,1,0:T(8,128)(2,1)} %get-tuple-element.11) | copy-start | bytes 2359300

commit v2 on v1

--- a/solution.py
+++ b/solution.py
@@ -35,21 +35,23 @@
 def kernel(
     q_in, do_in, kv_in, pk_in,
     out, dq, dkv_out, dp_out,
-    q2, do2, kv, p64, acc, mx, tot, lse, off, o16, dk, dv, g16, recv, recvp, psum, prem,
-    lsem, psem, kvs, kvr, pps, ppr, qsem, osem, gs, gr, gps, gpr, fsem,
+    q2, do2, kv, p64, acc, mx, tot, lse, off, o16, dk, dv, g16,
+    zr, zrp, gx, gxp, xr, xrp, psum, prem,
+    lsem, psem, kvxs, kvxr, kvzs, kvzr, ppxs, ppxr, ppzs, ppzr, qsem, osem,
+    gzs, gzr, gpzs, gpzr, gxs, gxr, gpxs, gpxr, fsem,
 ):
     s = lax.axis_index("seq")
     r = lax.axis_index("roll")
-    hs = s // 8
-    partner = N - 1 - s
-    high = jnp.maximum(s, partner)
-    need = (high // 2) * 2 + 1
+    x, z = s // 4, s % 4
+    hs = x // 2
+    top = jnp.maximum(x, 3 - x)
+    partner = 4 * (3 - x) + z
 
     barrier = pltpu.get_barrier_semaphore()
-    for d in range(1, N):
-        pl.semaphore_signal(barrier, inc=1, device_id={"seq": (s + d) % N}, device_id_type=MESH)
+    for d in range(1, 4):
+        pl.semaphore_signal(barrier, inc=1, device_id={"seq": (x + d) % 4 * 4 + z}, device_id_type=MESH)
+        pl.semaphore_signal(barrier, inc=1, device_id={"seq": 4 * x + (z + d) % 4}, device_id_type=MESH)
     pl.semaphore_signal(barrier, inc=1, device_id={"roll": 1 - r}, device_id_type=MESH)
-    pl.semaphore_wait(barrier, N)
 
     def remote(src, dst, ssem, rsem, **where):
         return pltpu.make_async_remote_copy(
@@ -57,53 +59,88 @@
             device_id=where, device_id_type=MESH,
         )
 
+    def kv_rows(j):
+        return kv.at[:, pl.ds(pl.multiple_of(PRM + j * BLK, 64), BLK), :]
+
+    def p_rows(zz, xx):
+        return kv.at[:, pl.ds(pl.multiple_of((zz * 4 + xx) * PB, PB), PB), :]
+
+    def p_column(zz):
+        return kv.at[:, pl.ds(pl.multiple_of(zz * 4 * PB, 4 * PB), 4 * PB), :]
+
     rows32 = pl.ds(pl.multiple_of(r * 32, 32), 32)
-    p_out = remote(pk_in, p64.at[:, :, rows32, :], psem.at[0], psem.at[1], roll=1 - r)
-    p_out.start()
     p_own = pltpu.make_async_copy(pk_in, p64.at[:, :, rows32, :], psem.at[2])
     p_own.start()
+    own_kv = pltpu.make_async_copy(kv_in.at[hs], kv_rows(s), lsem.at[2])
+    own_kv.start()
     own_q = pltpu.make_async_copy(q_in.at[hs], q2.at[0], lsem.at[0])
     own_q.start()
     own_do = pltpu.make_async_copy(do_in.at[hs], do2.at[0], lsem.at[1])
     own_do.start()
-
-    def kv_rows(j):
-        return kv.at[:, pl.ds(pl.multiple_of(PRM + j * BLK, 64), BLK), :]
-
-    def kv_copy(t):
-        return remote(kv_in.at[t // 8], kv_rows(s), kvs.at[t], kvr.at[s], seq=t)
-
-    def kv_wanted(t):
-        return s <= (jnp.maximum(t, N - 1 - t) // 2) * 2 + 1
-
-    own_kv = pltpu.make_async_copy(kv_in.at[hs], kv_rows(s), lsem.at[2])
-    own_kv.start()
-
-    def p_rows(j):
-        return kv.at[:, pl.ds(pl.multiple_of(j * PB, PB), PB), :]
-
-    def p_copy(t):
-        return remote(p64.at[t // 8], p_rows(s), pps.at[t], ppr.at[s], seq=t)
+    pl.semaphore_wait(barrier, 7)
+    p_out = remote(pk_in, p64.at[:, :, rows32, :], psem.at[0], psem.at[1], roll=1 - r)
+    p_out.start()
+
+    def kvx_copy(xx):
+        return remote(kv_in.at[xx // 2], kv_rows(s), kvxs.at[xx], kvxr.at[x], seq=4 * xx + z)
+
+    def px_copy(xx):
+        return remote(p64.at[xx // 2], p_rows(z, x), ppxs.at[xx], ppxr.at[x], seq=4 * xx + z)
+
+    def pz_copy(zz):
+        return remote(p_column(z), p_column(z), ppzs.at[zz], ppzr.at[z], seq=4 * x + zz)
+
+    def kvz_copy(zz, tile):
+        rows = kv_rows(4 * tile + z)
+        return remote(rows, rows, kvzs.at[zz, tile], kvzr.at[z, tile], seq=4 * x + zz)
+
+    def sees(xx):
+        return x <= jnp.maximum(xx, 3 - xx)
+
+    @pl.loop(1, 4)
+    def _(d):
+        xx = (x + d) % 4
+
+        @pl.when(sees(xx))
+        def _():
+            kvx_copy(xx).start()
 
     p_own.wait()
     p_out.wait_recv()
-    own_p = pltpu.make_async_copy(p64.at[hs], p_rows(s), lsem.at[3])
+    own_p = pltpu.make_async_copy(p64.at[hs], p_rows(z, x), lsem.at[3])
     own_p.start()
 
-    @pl.loop(1, N)
-    def _(d):
-        p_copy((s + d) % N).start()
+    @pl.loop(1, 4)
+    def _(d):
+        px_copy((x + d) % 4).start()
 
     q_out = remote(q_in.at[1 - hs], q2.at[1], qsem.at[0], qsem.at[1], seq=partner)
     q_out.start()
-
-    @pl.loop(1, N)
-    def _(d):
-        t = (s + d) % N
-
-        @pl.when(kv_wanted(t))
-        def _():
-            kv_copy(t).start()
+    acc[...] = jnp.zeros_like(acc)
+    mx[...] = jnp.full_like(mx, NEG)
+    tot[...] = jnp.zeros_like(tot)
+    own_p.wait()
+
+    @pl.loop(1, 4)
+    def _(d):
+        xx = (x + d) % 4
+        remote(p64.at[hs], p_rows(z, xx), ppxs.at[xx], ppxr.at[xx], seq=4 * xx + z).wait_recv()
+
+    @pl.loop(1, 4)
+    def _(d):
+        pz_copy((z + d) % 4).start()
+
+    own_kv.wait()
+
+    @pl.loop(0, top + 1)
+    def _(tile):
+        @pl.when(tile != x)
+        def _():
+            remote(kv_in.at[hs], kv_rows(4 * tile + z), kvxs.at[tile], kvxr.at[tile], seq=4 * tile + z).wait_recv()
+
+        @pl.loop(1, 4)
+        def _(d):
+            kvz_copy((z + d) % 4, tile).start()
 
     do_out = remote(do_in.at[1 - hs], do2.at[1], qsem.at[2], qsem.at[3], seq=partner)
     do_out.start()
@@ -129,56 +166,44 @@
         tot[b] = tot[b] * shrink + jnp.sum(lifted, 0, keepdims=True)
         acc[b] = acc[b] * shrink + dot(kv[1, rows, :], lifted.astype(bf16), TN)
 
-    acc[...] = jnp.zeros_like(acc)
-    mx[...] = jnp.full_like(mx, NEG)
-    tot[...] = jnp.zeros_like(tot)
     own_q.wait()
-    own_p.wait()
-
-    @pl.loop(1, N)
-    def _(d):
-        t = (s + d) % N
-        remote(p64.at[hs], p_rows(t), pps.at[t], ppr.at[t], seq=t).wait_recv()
-
-    @pl.loop(0, 2)
-    def _(b):
-        @pl.when(b == 1)
-        def _():
-            q_out.wait_recv()
-
-        forward_tile(b, 0, PRM, False)
+
+    @pl.loop(1, 4)
+    def _(d):
+        zz = (z + d) % 4
+        remote(p_column(zz), p_column(zz), ppzs.at[zz], ppzr.at[zz], seq=4 * x + zz).wait_recv()
 
     def wait_tile(tile):
-        @pl.loop(0, 4)
-        def _(i):
-            j = tile * 4 + i
-
-            @pl.when(j == s)
-            def _():
-                own_kv.wait()
-
-            @pl.when((j != s) & (j <= need))
-            def _():
-                remote(kv_in.at[hs], kv_rows(j), kvs.at[j], kvr.at[j], seq=j).wait_recv()
+        @pl.loop(1, 4)
+        def _(d):
+            zz = (z + d) % 4
+            rows = kv_rows(4 * tile + zz)
+            remote(rows, rows, kvzs.at[zz, tile], kvzr.at[zz, tile], seq=4 * x + zz).wait_recv()
 
     @pl.loop(0, 2)
     def _(b):
         blk = block_of(b)
         last = blk // 4
 
+        @pl.when(b == 1)
+        def _():
+            q_out.wait_recv()
+
+        forward_tile(b, 0, PRM, False)
+
         @pl.loop(0, last)
         def _(tile):
-            @pl.when((b == 0) | (tile > s // 4))
+            @pl.when((b == 0) | (tile > x))
             def _():
                 wait_tile(tile)
 
             forward_tile(b, PRM + tile * TILE, TILE, False)
 
-        @pl.when((b == 0) | (last > s // 4))
+        @pl.when((b == 0) | (last > x))
         def _():
             wait_tile(last)
 
-        @pl.loop(0, 1 + (blk % 4) // 2)
+        @pl.loop(0, 1 + z // 2)
         def _(half):
             forward_tile(b, PRM + last * TILE + half * HALF, HALF, True)
 
@@ -224,52 +249,85 @@
         g16[1, rows, :] = dv[rows, :].astype(bf16)
 
     def grad_rows(j):
-        return g16.at[:, pl.ds(pl.multiple_of(PRM + j * BLK, 64), BLK), :]
-
-    def grad_copy(j):
-        return remote(grad_rows(j), recv.at[s], gs.at[j], gr.at[s], seq=j)
-
-    own_g = pltpu.make_async_copy(grad_rows(s), recv.at[s], lsem.at[5])
+        return pl.ds(pl.multiple_of(PRM + j * BLK, 64), BLK)
+
+    def gz_copy(zz, tile):
+        rows = grad_rows(4 * tile + zz)
+        return remote(g16.at[:, rows, :], zr.at[z, tile], gzs.at[zz, tile], gzr.at[z, tile], seq=4 * x + zz)
+
+    def gx_copy(tile):
+        return remote(gx.at[tile], xr.at[x], gxs.at[tile], gxr.at[x], seq=4 * tile + z)
 
     def send_tile(tile):
         finish_rows(PRM + tile * TILE, TILE)
 
-        @pl.loop(0, 4)
-        def _(i):
-            j = tile * 4 + i
-
-            @pl.when(j == s)
-            def _():
-                own_g.start()
-
-            @pl.when((j != s) & (j <= high))
-            def _():
-                grad_copy(j).start()
-
-    def gp_rows(t):
-        return g16.at[:, pl.ds(pl.multiple_of(t * PB, PB), PB), :]
-
-    def gp_copy(t):
-        return remote(gp_rows(t), recvp.at[s], gps.at[t], gpr.at[s], seq=t)
-
-    own_gp = pltpu.make_async_copy(gp_rows(s), recvp.at[s], lsem.at[6])
+        @pl.loop(1, 4)
+        def _(d):
+            gz_copy((z + d) % 4, tile).start()
+
+    def pass_tile(tile):
+        rows = grad_rows(4 * tile + z)
+        total = g16[:, rows, :].astype(f32)
+        for d in range(1, 4):
+            zz = (z + d) % 4
+            remote(g16.at[:, rows, :], zr.at[zz, tile], gzs.at[zz, tile], gzr.at[zz, tile], seq=4 * x + zz).wait_recv()
+            total = total + zr[zz, tile].astype(f32)
+
+        @pl.when(tile == x)
+        def _():
+            xr[x] = total.astype(bf16)
+
+        @pl.when(tile != x)
+        def _():
+            gx[tile] = total.astype(bf16)
+            gx_copy(tile).start()
+
+    def column(zz):
+        return pl.ds(pl.multiple_of(zz * 4 * PB, 4 * PB), 4 * PB)
+
+    def gpz_copy(zz):
+        return remote(g16.at[:, column(zz), :], zrp.at[z], gpzs.at[zz], gpzr.at[z], seq=4 * x + zz)
+
+    def gpx_copy(xx):
+        rows = pl.ds(pl.multiple_of(xx * PB, PB), PB)
+        return remote(gxp.at[:, rows, :], xrp.at[x], gpxs.at[xx], gpxr.at[x], seq=4 * xx + z)
+
+    def send_prompt():
+        finish_rows(0, PRM)
+
+        @pl.loop(1, 4)
+        def _(d):
+            gpz_copy((z + d) % 4).start()
+
+    def pass_prompt():
+        total = g16[:, column(z), :].astype(f32)
+        for d in range(1, 4):
+            zz = (z + d) % 4
+            remote(g16.at[:, column(z), :], zrp.at[zz], gpzs.at[zz], gpzr.at[zz], seq=4 * x + zz).wait_recv()
+            total = total + zrp[zz].astype(f32)
+        gxp[...] = total.astype(bf16)
+
+        @pl.loop(1, 4)
+        def _(d):
+            gpx_copy((x + d) % 4).start()
+
+        xrp[x] = gxp[:, pl.ds(pl.multiple_of(x * PB, PB), PB), :]
+
     dq_out = remote(o16.at[3], dq.at[hs], osem.at[2], osem.at[3], seq=partner)
 
     @pl.loop(0, 2)
     def _(i):
         b = 1 - i
-        blk = block_of(b)
-        last = blk // 4
+        last = jnp.where(b == 0, x, 3 - x)
         backward_tile(b, 0, PRM, False)
 
         @pl.when(b == 0)
         def _():
-            finish_rows(0, PRM)
-            own_gp.start()
-
-            @pl.loop(1, N)
-            def _(d):
-                gp_copy((s + d) % N).start()
+            send_prompt()
+
+            @pl.loop(x + 1, 4 - x)
+            def _(tile):
+                pass_tile(tile)
 
         @pl.loop(0, last)
         def _(tile):
@@ -279,60 +337,69 @@
             def _():
                 send_tile(tile)
 
-        @pl.loop(0, 1 + (blk % 4) // 2)
+                @pl.when(tile == 0)
+                def _():
+                    pass_prompt()
+
+                @pl.when(tile > 0)
+                def _():
+                    pass_tile(tile - 1)
+
+        @pl.loop(0, 1 + z // 2)
         def _(half):
             backward_tile(b, PRM + last * TILE + half * HALF, HALF, True)
 
+        @pl.when(b == 0)
+        def _():
+            send_tile(last)
+
         o16[2 + b] = (acc[b] * SCALE).T.astype(bf16)
 
-        @pl.when(b == 0)
-        def _():
-            send_tile(last)
-
         @pl.when(b == 1)
         def _():
             dq_out.start()
 
-            @pl.loop(s // 4 + 1, partner // 4 + 1)
+            @pl.loop(x + 1, 4 - x)
             def _(tile):
                 send_tile(tile)
 
     own_dq = pltpu.make_async_copy(o16.at[2], dq.at[hs], lsem.at[7])
     own_dq.start()
 
-    own_gp.wait()
-
-    @pl.loop(1, N)
-    def _(d):
-        t = (s + d) % N
-        remote(gp_rows(t), recvp.at[t], gps.at[t], gpr.at[t], seq=t).wait_recv()
+    @pl.when(x == 0)
+    def _():
+        pass_prompt()
+
+    @pl.when(x > 0)
+    def _():
+        pass_tile(x - 1)
+
+    pass_tile(x)
+
+    @pl.loop(1, 4)
+    def _(d):
+        xx = (x + d) % 4
+        remote(gxp.at[:, pl.ds(0, PB), :], xrp.at[xx], gpxs.at[xx], gpxr.at[xx], seq=4 * xx + z).wait_recv()
 
     for h in range(2):
-        total = recvp[8 * h].astype(f32)
-        for i in range(1, 8):
-            total = total + recvp[8 * h + i].astype(f32)
-        psum[h] = total
+        psum[h] = xrp[2 * h].astype(f32) + xrp[2 * h + 1].astype(f32)
     theirs = pl.ds(pl.multiple_of((1 - r) * 32, 32), 32)
     f_out = remote(psum.at[:, :, theirs, :], prem, fsem.at[0], fsem.at[1], roll=1 - r)
     f_out.start()
 
-    own_g.wait()
-
-    @pl.loop(1, N)
-    def _(d):
-        t = (s + d) % N
-
-        @pl.when(s <= jnp.maximum(t, N - 1 - t))
-        def _():
-            remote(grad_rows(s), recv.at[t], gs.at[t], gr.at[t], seq=t).wait_recv()
-
-    total0 = jnp.zeros(recv.shape[1:], f32)
-    total1 = jnp.zeros(recv.shape[1:], f32)
-    for i in range(8):
-        total0 = total0 + jnp.where(s <= N - 1 - i, recv[i].astype(f32), 0.0)
-        total1 = total1 + jnp.where(s <= 8 + i, recv[8 + i].astype(f32), 0.0)
-    dkv_out[0] = total0.astype(bf16)
-    dkv_out[1] = total1.astype(bf16)
+    @pl.loop(1, 4)
+    def _(d):
+        xx = (x + d) % 4
+
+        @pl.when(sees(xx))
+        def _():
+            remote(gx.at[xx], xr.at[xx], gxs.at[xx], gxr.at[xx], seq=4 * xx + z).wait_recv()
+
+    for h in range(2):
+        total = jnp.zeros(xr.shape[1:], f32)
+        for xx in (2 * h, 2 * h + 1):
+            total = total + jnp.where(x <= max(xx, 3 - xx), xr[xx].astype(f32), 0.0)
+        dkv_out[h] = total.astype(bf16)
     f_out.wait_recv()
     dp_out[...] = (psum[:, :, rows32, :] + prem[...]).astype(bf16)
 
@@ -345,19 +412,27 @@
     own_out.wait()
     own_dq.wait()
 
-    @pl.loop(1, N)
-    def _(d):
-        t = (s + d) % N
-        p_copy(t).wait_send()
-        gp_copy(t).wait_send()
-
-        @pl.when(kv_wanted(t))
-        def _():
-            kv_copy(t).wait_send()
-
-        @pl.when(t <= high)
-        def _():
-            grad_copy(t).wait_send()
+    @pl.loop(1, 4)
+    def _(d):
+        xx = (x + d) % 4
+        zz = (z + d) % 4
+        px_copy(xx).wait_send()
+        pz_copy(zz).wait_send()
+        gpz_copy(zz).wait_send()
+        gpx_copy(xx).wait_send()
+
+        @pl.when(sees(xx))
+        def _():
+            kvx_copy(xx).wait_send()
+
+        @pl.when(xx <= top)
+        def _():
+            gx_copy(xx).wait_send()
+
+        @pl.loop(0, top + 1)
+        def _(tile):
+            kvz_copy(zz, tile).wait_send()
+            gz_copy(zz, tile).wait_send()
 
 
 def attention(q_rows, do_rows, kv_rows, prompt_rows):
@@ -388,22 +463,34 @@
             pltpu.VMEM((PRM + N * BLK, HD), f32),
             pltpu.VMEM((PRM + N * BLK, HD), f32),
             pltpu.VMEM((2, PRM + N * BLK, HD), bf16),
-            pltpu.VMEM((N, 2, BLK, HD), bf16),
-            pltpu.VMEM((N, 2, PB, HD), bf16),
+            pltpu.VMEM((4, 4, 2, BLK, HD), bf16),
+            pltpu.VMEM((4, 2, 4 * PB, HD), bf16),
+            pltpu.VMEM((4, 2, BLK, HD), bf16),
+            pltpu.VMEM((2, 4 * PB, HD), bf16),
+            pltpu.VMEM((4, 2, BLK, HD), bf16),
+            pltpu.VMEM((4, 2, PB, HD), bf16),
             pltpu.VMEM((2, 2, PB, HD), f32),
             pltpu.VMEM((2, 2, 32, HD), f32),
             dma((8,)),
             dma((3,)),
-            dma((N,)),
-            dma((N,)),
-            dma((N,)),
-            dma((N,)),
-            dma((4,)),
-            dma((4,)),
-            dma((N,)),
-            dma((N,)),
-            dma((N,)),
-            dma((N,)),
+            dma((4,)),
+            dma((4,)),
+            dma((4, 4)),
+            dma((4, 4)),
+            dma((4,)),
+            dma((4,)),
+            dma((4,)),
+            dma((4,)),
+            dma((4,)),
+            dma((4,)),
+            dma((4, 4)),
+            dma((4, 4)),
+            dma((4,)),
+            dma((4,)),
+            dma((4,)),
+            dma((4,)),
+            dma((4,)),
+            dma((4,)),
             dma((2,)),
         ],
         compiler_params=pltpu.CompilerParams(

time: 119 us -> 105 us (0.88)
  the two profiles are of different devices: /device:TPU:0 before, /device:TPU:6 now
where the time goes in v2:
time: 105 us
  Pallas kernels  91.6 us (87%)
  local copies, waits for them, and re-layouts  6.34 us (6%)
  other arithmetic  5.17 us (5%)
  between operations  1.47 us (1%)
    pallas_call x1, Pallas kernels, attention(): pl.pallas_call(kernel, out_shape=[jax.ShapeDtypeStruct((2, RB, HD), bf16)...  91.6 us
    unnamed x16, local copies, waits for them, and re-layouts  4.56 us
    reshape x1, other arithmetic, merged(): return rows.transpose(1, 0, 2, 3).reshape(1, BLK, 2 * PG, HD)  2.33 us

profile of v2, /device:TPU:6, one launch (start us, length us, event | category | flops | bytes accessed | tf_op | source)
XLA Modules:
  0.0 104.6 jit_solution(764301703088007343)
XLA Ops:
  0.6 0.0 copy-start
  0.6 0.0 copy-start.2
  1.4 0.7 copy_bitcast_fusion.3
  2.2 0.6 maximum_bitcast_fusion.1.pk_in
  2.8 0.9 copy.15
  3.7 0.9 copy.16
  4.6 0.7 maximum_bitcast_fusion.kv_in
  5.3 0.0 copy-done
  5.3 0.0 copy-done.2
  5.3 1.5 %fusion.1 = (bf16[2,1536,128]{2,1,0:T(8,128)(2,1)}, bf16[2,1536,128]{2,1,0:T(8,128)(2,1)}) fusion(pred[192]{0:T(512)(128)(4,1)S(1)} %add_compare_fusion, bf16[1,192,16,128]{3,2,1,0:T(8,128)(2,1)S(1)} %copy-done, bf16[1,192,16,128]{3,2,1,0:T(8,128)(2,1)S(1)} %copy-done.2), kind=kLoop, calls=%fused_computation.5 | loop fusion | flops 393216 | bytes 3145920 | tf_op jit(solution)/shard_map/reshape | solution.py:514
  6.8 91.6 %shard_map.118 = (bf16[2,1536,128]{2,1,0:T(8,128)(2,1)}, bf16[2,1536,128]{2,1,0:T(8,128)(2,1)}, bf16[2,2,192,128]{3,2,1,0:T(8,128)(2,1)}, bf16[2,2,32,128]{3,2,1,0:T(8,128)(2,1)}) custom-call(bf16[2,1536,128]{2,1,0:T(8,128)(2,1)} %get-tuple-element.27.q_in, bf16[2,1536,128]{2,1,0:T(8,128)(2,1)} %get-tuple-element.26.do_in, ...), custom_call_target="tpu_custom_call" | custom-call | tf_op jit(solution)/shard_map/pallas_call | solution.py:442
  98.5 0.0 copy-start.4
  98.5 0.0 copy-start.3
  98.5 2.3 %copy_bitcast_fusion.1 = bf16[1,192,16,128]{3,2,1,0:T(8,128)(2,1)} fusion(bf16[2,1536,128]{2,1,0:T(8,128)(2,1)} %get-tuple-element.10, pred[192]{0:T(512)(128)(4,1)S(1)} %add_compare_fusion), kind=kLoop, calls=%fused_computation.3 | loop fusion | flops 393216 | bytes 1573056 | tf_op jit(solution)/shard_map/reshape | solution.py:510
  100.8 0.0 copy-done.4
  100.8 0.0 copy-start.1
  100.9 0.6 copy.24
  101.5 0.6 copy.23
  102.1 0.0 copy-done.3
  102.1 0.7 copy.22
  102.9 0.7 copy.21
  103.6 0.0 copy-done.1
  103.6 1.0 copy_bitcast_fusion
  (3 shorter events, 0.0 us)
Async XLA Ops:
  0.6 4.7 %copy-start = (bf16[1,192,16,128]{3,2,1,0:T(8,128)(2,1)S(1)}, bf16[1,192,16,128]{3,2,1,0:T(8,128)(2,1)}, u32[]{:S(2)}) copy-start(bf16[1,192,16,128]{3,2,1,0:T(8,128)(2,1)} %param.7) | copy-start | bytes 2359300
  0.6 4.7 %copy-start.2 = (bf16[1,192,16,128]{3,2,1,0:T(8,128)(2,1)S(1)}, bf16[1,192,16,128]{3,2,1,0:T(8,128)(2,1)}, u32[]{:S(2)}) copy-start(bf16[1,192,16,128]{3,2,1,0:T(8,128)(2,1)} %param.12) | copy-start | bytes 2359300
  98.5 2.3 %copy-start.4 = (bf16[2,2,32,128]{3,2,1,0:T(8,128)(2,1)S(1)}, bf16[2,2,32,128]{3,2,1,0:T(8,128)(2,1)}, u32[]{:S(2)}) copy-start(bf16[2,2,32,128]{3,2,1,0:T(8,128)(2,1)} %get-tuple-element.13) | copy-start | bytes 98308
  98.5 3.6 %copy-start.3 = (bf16[2,2,192,128]{3,2,1,0:T(8,128)(2,1)S(1)}, bf16[2,2,192,128]{3,2,1,0:T(8,128)(2,1)}, u32[]{:S(2)}) copy-start(bf16[2,2,192,128]{3,2,1,0:T(8,128)(2,1)} %get-tuple-element.12) | copy-start | bytes 589828
  100.8 2.8 %copy-start.1 = (bf16[2,1536,128]{2,1,0:T(8,128)(2,1)S(1)}, bf16[2,1536,128]{2,1,0:T(8,128)(2,1)}, u32[]{:S(2)}) copy-start(bf16[2,1536,128]{2,1,0:T(8,128)(2,1)} %get-tuple-element.11) | copy-start | bytes 2359300

commit v3 on v2

--- a/solution.py
+++ b/solution.py
@@ -11,7 +11,6 @@
 N = 16
 BLK = 192
 PRM = 1024
-PB = 64
 HD = 128
 PG = 8
 RB = BLK * PG
@@ -35,10 +34,10 @@
 def kernel(
     q_in, do_in, kv_in, pk_in,
     out, dq, dkv_out, dp_out,
-    q2, do2, kv, p64, acc, mx, tot, lse, off, o16, dk, dv, g16,
-    zr, zrp, gx, gxp, xr, xrp, psum, prem,
-    lsem, psem, kvxs, kvxr, kvzs, kvzr, ppxs, ppxr, ppzs, ppzr, qsem, osem,
-    gzs, gzr, gpzs, gpzr, gxs, gxr, gpxs, gpxr, fsem,
+    q2, do2, kv, acc, mx, tot, lse, off, o16, dk, dv, g16,
+    zr, yrp, gyp, zrp, gx, gxp, xr, xrp,
+    lsem, kvxs, kvxr, kvzs, kvzr, ppxs, ppxr, ppzs, ppzr, ppys, ppyr, qsem, osem,
+    gzs, gzr, gpys, gpzs, gpzr, gxs, gxr, gpxs, gpxr,
 ):
     s = lax.axis_index("seq")
     r = lax.axis_index("roll")
@@ -62,15 +61,14 @@
     def kv_rows(j):
         return kv.at[:, pl.ds(pl.multiple_of(PRM + j * BLK, 64), BLK), :]
 
-    def p_rows(zz, xx):
-        return kv.at[:, pl.ds(pl.multiple_of((zz * 4 + xx) * PB, PB), PB), :]
-
-    def p_column(zz):
-        return kv.at[:, pl.ds(pl.multiple_of(zz * 4 * PB, 4 * PB), 4 * PB), :]
-
-    rows32 = pl.ds(pl.multiple_of(r * 32, 32), 32)
-    p_own = pltpu.make_async_copy(pk_in, p64.at[:, :, rows32, :], psem.at[2])
-    p_own.start()
+    def p_rows(xx):
+        return kv.at[:, pl.ds(pl.multiple_of(r * 512 + z * 128 + xx * 32, 32), 32), :]
+
+    def p_column(rr, zz):
+        return kv.at[:, pl.ds(pl.multiple_of(rr * 512 + zz * 128, 128), 128), :]
+
+    own_p = pltpu.make_async_copy(pk_in.at[hs], p_rows(x), lsem.at[3])
+    own_p.start()
     own_kv = pltpu.make_async_copy(kv_in.at[hs], kv_rows(s), lsem.at[2])
     own_kv.start()
     own_q = pltpu.make_async_copy(q_in.at[hs], q2.at[0], lsem.at[0])
@@ -78,17 +76,18 @@
     own_do = pltpu.make_async_copy(do_in.at[hs], do2.at[0], lsem.at[1])
     own_do.start()
     pl.semaphore_wait(barrier, 7)
-    p_out = remote(pk_in, p64.at[:, :, rows32, :], psem.at[0], psem.at[1], roll=1 - r)
-    p_out.start()
 
     def kvx_copy(xx):
         return remote(kv_in.at[xx // 2], kv_rows(s), kvxs.at[xx], kvxr.at[x], seq=4 * xx + z)
 
     def px_copy(xx):
-        return remote(p64.at[xx // 2], p_rows(z, x), ppxs.at[xx], ppxr.at[x], seq=4 * xx + z)
+        return remote(pk_in.at[xx // 2], p_rows(x), ppxs.at[xx], ppxr.at[x], seq=4 * xx + z)
 
     def pz_copy(zz):
-        return remote(p_column(z), p_column(z), ppzs.at[zz], ppzr.at[z], seq=4 * x + zz)
+        return remote(p_column(r, z), p_column(r, z), ppzs.at[zz], ppzr.at[z], seq=4 * x + zz)
+
+    def py_copy(zz):
+        return remote(p_column(r, zz), p_column(r, zz), ppys.at[zz], ppyr.at[zz], roll=1 - r)
 
     def kvz_copy(zz, tile):
         rows = kv_rows(4 * tile + z)
@@ -99,20 +98,15 @@
 
     @pl.loop(1, 4)
     def _(d):
+        px_copy((x + d) % 4).start()
+
+    @pl.loop(1, 4)
+    def _(d):
         xx = (x + d) % 4
 
         @pl.when(sees(xx))
         def _():
             kvx_copy(xx).start()
-
-    p_own.wait()
-    p_out.wait_recv()
-    own_p = pltpu.make_async_copy(p64.at[hs], p_rows(z, x), lsem.at[3])
-    own_p.start()
-
-    @pl.loop(1, 4)
-    def _(d):
-        px_copy((x + d) % 4).start()
 
     q_out = remote(q_in.at[1 - hs], q2.at[1], qsem.at[0], qsem.at[1], seq=partner)
     q_out.start()
@@ -124,12 +118,13 @@
     @pl.loop(1, 4)
     def _(d):
         xx = (x + d) % 4
-        remote(p64.at[hs], p_rows(z, xx), ppxs.at[xx], ppxr.at[xx], seq=4 * xx + z).wait_recv()
+        remote(pk_in.at[hs], p_rows(xx), ppxs.at[xx], ppxr.at[xx], seq=4 * xx + z).wait_recv()
 
     @pl.loop(1, 4)
     def _(d):
         pz_copy((z + d) % 4).start()
 
+    py_copy(z).start()
     own_kv.wait()
 
     @pl.loop(0, top + 1)
@@ -141,6 +136,12 @@
         @pl.loop(1, 4)
         def _(d):
             kvz_copy((z + d) % 4, tile).start()
+
+    @pl.loop(1, 4)
+    def _(d):
+        zz = (z + d) % 4
+        remote(p_column(r, zz), p_column(r, zz), ppzs.at[zz], ppzr.at[zz], seq=4 * x + zz).wait_recv()
+        py_copy(zz).start()
 
     do_out = remote(do_in.at[1 - hs], do2.at[1], qsem.at[2], qsem.at[3], seq=partner)
     do_out.start()
@@ -168,11 +169,6 @@
 
     own_q.wait()
 
-    @pl.loop(1, 4)
-    def _(d):
-        zz = (z + d) % 4
-        remote(p_column(zz), p_column(zz), ppzs.at[zz], ppzr.at[zz], seq=4 * x + zz).wait_recv()
-
     def wait_tile(tile):
         @pl.loop(1, 4)
         def _(d):
@@ -189,7 +185,17 @@
         def _():
             q_out.wait_recv()
 
-        forward_tile(b, 0, PRM, False)
+        @pl.loop(0, 2)
+        def _(i):
+            half = (r + i) % 2
+
+            @pl.when((b == 0) & (i == 1))
+            def _():
+                @pl.loop(0, 4)
+                def _(zz):
+                    remote(p_column(half, zz), p_column(half, zz), ppys.at[zz], ppyr.at[zz], roll=half).wait_recv()
+
+            forward_tile(b, half * 512, 512, False)
 
         @pl.loop(0, last)
         def _(tile):
@@ -282,28 +288,33 @@
             gx[tile] = total.astype(bf16)
             gx_copy(tile).start()
 
-    def column(zz):
-        return pl.ds(pl.multiple_of(zz * 4 * PB, 4 * PB), 4 * PB)
+    mine = pl.ds(pl.multiple_of(r * 512, 512), 512)
+    theirs = pl.ds(pl.multiple_of((1 - r) * 512, 512), 512)
+    gpy_out = remote(g16.at[:, theirs, :], yrp, gpys.at[0], gpys.at[1], roll=1 - r)
 
     def gpz_copy(zz):
-        return remote(g16.at[:, column(zz), :], zrp.at[z], gpzs.at[zz], gpzr.at[z], seq=4 * x + zz)
+        rows = pl.ds(pl.multiple_of(zz * 128, 128), 128)
+        return remote(gyp.at[:, rows, :], zrp.at[z], gpzs.at[zz], gpzr.at[z], seq=4 * x + zz)
 
     def gpx_copy(xx):
-        rows = pl.ds(pl.multiple_of(xx * PB, PB), PB)
+        rows = pl.ds(pl.multiple_of(xx * 32, 32), 32)
         return remote(gxp.at[:, rows, :], xrp.at[x], gpxs.at[xx], gpxr.at[x], seq=4 * xx + z)
 
-    def send_prompt():
-        finish_rows(0, PRM)
+    def pass_rolls():
+        gpy_out.wait_recv()
+        gyp[0] = (dk[mine, :] * SCALE + yrp[0].astype(f32)).astype(bf16)
+        gyp[1] = (dv[mine, :] + yrp[1].astype(f32)).astype(bf16)
 
         @pl.loop(1, 4)
         def _(d):
             gpz_copy((z + d) % 4).start()
 
     def pass_prompt():
-        total = g16[:, column(z), :].astype(f32)
+        rows = pl.ds(pl.multiple_of(z * 128, 128), 128)
+        total = gyp[:, rows, :].astype(f32)
         for d in range(1, 4):
             zz = (z + d) % 4
-            remote(g16.at[:, column(z), :], zrp.at[zz], gpzs.at[zz], gpzr.at[zz], seq=4 * x + zz).wait_recv()
+            remote(gyp.at[:, rows, :], zrp.at[zz], gpzs.at[zz], gpzr.at[zz], seq=4 * x + zz).wait_recv()
             total = total + zrp[zz].astype(f32)
         gxp[...] = total.astype(bf16)
 
@@ -311,81 +322,84 @@
         def _(d):
             gpx_copy((x + d) % 4).start()
 
-        xrp[x] = gxp[:, pl.ds(pl.multiple_of(x * PB, PB), PB), :]
+        xrp[x] = gxp[:, pl.ds(pl.multiple_of(x * 32, 32), 32), :]
 
     dq_out = remote(o16.at[3], dq.at[hs], osem.at[2], osem.at[3], seq=partner)
 
-    @pl.loop(0, 2)
+    low = jnp.minimum(x, 3 - x)
+    early = 3 - 2 * low
+    later = jnp.where(x < 2, 1, 0)
+
+    @pl.loop(0, 7)
     def _(i):
-        b = 1 - i
-        last = jnp.where(b == 0, x, 3 - x)
-        backward_tile(b, 0, PRM, False)
-
-        @pl.when(b == 0)
-        def _():
-            send_prompt()
-
-            @pl.loop(x + 1, 4 - x)
-            def _(tile):
-                pass_tile(tile)
-
-        @pl.loop(0, last)
-        def _(tile):
+        k = i - early - 2
+        rest = k >= 0
+        first = i < early
+        prompt = (i >= early) & (k < 0)
+        second = k > low
+        b = jnp.where(first, later, jnp.where(prompt, early + 1 - i, jnp.where(second, 0, 1)))
+        tile = jnp.where(first, 3 - low - i, jnp.where(second, k - low - 1, jnp.maximum(k, 0)))
+        diagonal = (i == 0) | (rest & (b != later) & (tile == low))
+
+        @pl.when(prompt)
+        def _():
+            backward_tile(b, 0, PRM, False)
+
+        @pl.when((first | rest) & jnp.logical_not(diagonal))
+        def _():
             backward_tile(b, PRM + tile * TILE, TILE, False)
 
-            @pl.when(b == 0)
+        @pl.when(diagonal)
+        def _():
+            @pl.loop(0, 1 + z // 2)
+            def _(half):
+                backward_tile(b, PRM + tile * TILE + half * HALF, HALF, True)
+
+        @pl.when(first | (rest & second))
+        def _():
+            send_tile(tile)
+
+        @pl.when((i > 0) & (i <= early))
+        def _():
+            pass_tile(4 - low - i)
+
+        @pl.when(i == early + 1)
+        def _():
+            finish_rows(0, PRM)
+            gpy_out.start()
+
+        @pl.when(k == 0)
+        def _():
+            pass_rolls()
+
+        @pl.when(k == 1)
+        def _():
+            pass_prompt()
+
+        @pl.when(k == low)
+        def _():
+            o16[3] = (acc[1] * SCALE).T.astype(bf16)
+            dq_out.start()
+
+        @pl.when(k == 2 * low + 1)
+        def _():
+            o16[2] = (acc[0] * SCALE).T.astype(bf16)
+
+            @pl.when(low == 1)
             def _():
-                send_tile(tile)
-
-                @pl.when(tile == 0)
-                def _():
-                    pass_prompt()
-
-                @pl.when(tile > 0)
-                def _():
-                    pass_tile(tile - 1)
-
-        @pl.loop(0, 1 + z // 2)
-        def _(half):
-            backward_tile(b, PRM + last * TILE + half * HALF, HALF, True)
-
-        @pl.when(b == 0)
-        def _():
-            send_tile(last)
-
-        o16[2 + b] = (acc[b] * SCALE).T.astype(bf16)
-
-        @pl.when(b == 1)
-        def _():
-            dq_out.start()
-
-            @pl.loop(x + 1, 4 - x)
-            def _(tile):
-                send_tile(tile)
+                pass_tile(0)
 
     own_dq = pltpu.make_async_copy(o16.at[2], dq.at[hs], lsem.at[7])
     own_dq.start()
-
-    @pl.when(x == 0)
-    def _():
-        pass_prompt()
-
-    @pl.when(x > 0)
-    def _():
-        pass_tile(x - 1)
-
-    pass_tile(x)
+    pass_tile(low)
 
     @pl.loop(1, 4)
     def _(d):
         xx = (x + d) % 4
-        remote(gxp.at[:, pl.ds(0, PB), :], xrp.at[xx], gpxs.at[xx], gpxr.at[xx], seq=4 * xx + z).wait_recv()
+        remote(gxp.at[:, pl.ds(0, 32), :], xrp.at[xx], gpxs.at[xx], gpxr.at[xx], seq=4 * xx + z).wait_recv()
 
     for h in range(2):
-        psum[h] = xrp[2 * h].astype(f32) + xrp[2 * h + 1].astype(f32)
-    theirs = pl.ds(pl.multiple_of((1 - r) * 32, 32), 32)
-    f_out = remote(psum.at[:, :, theirs, :], prem, fsem.at[0], fsem.at[1], roll=1 - r)
-    f_out.start()
+        dp_out[h] = (xrp[2 * h].astype(f32) + xrp[2 * h + 1].astype(f32)).astype(bf16)
 
     @pl.loop(1, 4)
     def _(d):
@@ -400,15 +414,13 @@
         for xx in (2 * h, 2 * h + 1):
             total = total + jnp.where(x <= max(xx, 3 - xx), xr[xx].astype(f32), 0.0)
         dkv_out[h] = total.astype(bf16)
-    f_out.wait_recv()
-    dp_out[...] = (psum[:, :, rows32, :] + prem[...]).astype(bf16)
-
-    p_out.wait_send()
+
+    py_copy(z).wait_send()
+    gpy_out.wait_send()
     q_out.wait_send()
     do_out.wait_send()
     out_out.wait()
     dq_out.wait()
-    f_out.wait_send()
     own_out.wait()
     own_dq.wait()
 
@@ -418,6 +430,7 @@
         zz = (z + d) % 4
         px_copy(xx).wait_send()
         pz_copy(zz).wait_send()
+        py_copy(zz).wait_send()
         gpz_copy(zz).wait_send()
         gpx_copy(xx).wait_send()
 
@@ -453,7 +466,6 @@
             pltpu.VMEM((2, RB, HD), bf16),
             pltpu.VMEM((2, RB, HD), bf16),
             pltpu.VMEM((2, PRM + N * BLK, HD), bf16),
-            pltpu.VMEM((2, 2, PB, HD), bf16),
             pltpu.VMEM((2, HD, RB), f32),
             pltpu.VMEM((2, 1, RB), f32),
             pltpu.VMEM((2, 1, RB), f32),
@@ -464,15 +476,14 @@
             pltpu.VMEM((PRM + N * BLK, HD), f32),
             pltpu.VMEM((2, PRM + N * BLK, HD), bf16),
             pltpu.VMEM((4, 4, 2, BLK, HD), bf16),
-            pltpu.VMEM((4, 2, 4 * PB, HD), bf16),
+            pltpu.VMEM((2, 512, HD), bf16),
+            pltpu.VMEM((2, 512, HD), bf16),
+            pltpu.VMEM((4, 2, 128, HD), bf16),
             pltpu.VMEM((4, 2, BLK, HD), bf16),
-            pltpu.VMEM((2, 4 * PB, HD), bf16),
+            pltpu.VMEM((2, 128, HD), bf16),
             pltpu.VMEM((4, 2, BLK, HD), bf16),
-            pltpu.VMEM((4, 2, PB, HD), bf16),
-            pltpu.VMEM((2, 2, PB, HD), f32),
-            pltpu.VMEM((2, 2, 32, HD), f32),
+            pltpu.VMEM((4, 2, 32, HD), bf16),
             dma((8,)),
-            dma((3,)),
             dma((4,)),
             dma((4,)),
             dma((4, 4)),
@@ -483,15 +494,17 @@
             dma((4,)),
             dma((4,)),
             dma((4,)),
+            dma((4,)),
+            dma((4,)),
             dma((4, 4)),
             dma((4, 4)),
-            dma((4,)),
-            dma((4,)),
-            dma((4,)),
-            dma((4,)),
-            dma((4,)),
-            dma((4,)),
             dma((2,)),
+            dma((4,)),
+            dma((4,)),
+            dma((4,)),
+            dma((4,)),
+            dma((4,)),
+            dma((4,)),
         ],
         compiler_params=pltpu.CompilerParams(
             collective_id=0, has_side_effects=True, vmem_limit_bytes=58 * 2**20

time: 105 us -> 98 us (0.933)
  the two profiles are of different devices: /device:TPU:6 before, /device:TPU:0 now
where the time goes in v3:
time: 98 us; the launch traced here: 97.8 us
  Pallas kernels  84.8 us (87%)
  local copies, waits for them, and re-layouts  6.34 us (6%)
  other arithmetic  5.17 us (5%)
  between operations  1.47 us (2%)
    pallas_call x1, Pallas kernels, attention(): pl.pallas_call(kernel, out_shape=[jax.ShapeDtypeStruct((2, RB, HD), bf16)...  84.8 us
    unnamed x16, local copies, waits for them, and re-layouts  4.56 us
    reshape x1, other arithmetic, merged(): return rows.transpose(1, 0, 2, 3).reshape(1, BLK, 2 * PG, HD)  2.33 us

profile of v3, /device:TPU:0, one launch (start us, length us, event | category | flops | bytes accessed | tf_op | source)
XLA Modules:
  0.0 97.8 jit_solution(7198641607043364141)
XLA Ops:
  0.6 0.0 copy-start
  0.6 0.0 copy-start.2
  1.4 0.7 copy_bitcast_fusion.3
  2.2 0.6 maximum_bitcast_fusion.1.pk_in
  2.8 0.9 copy.15
  3.7 0.9 copy.16
  4.6 0.7 maximum_bitcast_fusion.kv_in
  5.3 0.0 copy-done
  5.3 0.0 copy-done.2
  5.3 1.5 %fusion.1 = (bf16[2,1536,128]{2,1,0:T(8,128)(2,1)}, bf16[2,1536,128]{2,1,0:T(8,128)(2,1)}) fusion(pred[192]{0:T(512)(128)(4,1)S(1)} %add_compare_fusion, bf16[1,192,16,128]{3,2,1,0:T(8,128)(2,1)S(1)} %copy-done, bf16[1,192,16,128]{3,2,1,0:T(8,128)(2,1)S(1)} %copy-done.2), kind=kLoop, calls=%fused_computation.5 | loop fusion | flops 393216 | bytes 3145920 | tf_op jit(solution)/shard_map/reshape | solution.py:527
  6.8 84.8 %shard_map.118 = (bf16[2,1536,128]{2,1,0:T(8,128)(2,1)}, bf16[2,1536,128]{2,1,0:T(8,128)(2,1)}, bf16[2,2,192,128]{3,2,1,0:T(8,128)(2,1)}, bf16[2,2,32,128]{3,2,1,0:T(8,128)(2,1)}) custom-call(bf16[2,1536,128]{2,1,0:T(8,128)(2,1)} %get-tuple-element.27.q_in, bf16[2,1536,128]{2,1,0:T(8,128)(2,1)} %get-tuple-element.26.do_in, ...), custom_call_target="tpu_custom_call" | custom-call | tf_op jit(solution)/shard_map/pallas_call | solution.py:455
  91.7 0.0 copy-start.4
  91.7 0.0 copy-start.3
  91.7 2.3 %copy_bitcast_fusion.1 = bf16[1,192,16,128]{3,2,1,0:T(8,128)(2,1)} fusion(bf16[2,1536,128]{2,1,0:T(8,128)(2,1)} %get-tuple-element.10, pred[192]{0:T(512)(128)(4,1)S(1)} %add_compare_fusion), kind=kLoop, calls=%fused_computation.3 | loop fusion | flops 393216 | bytes 1573056 | tf_op jit(solution)/shard_map/reshape | solution.py:523
  94.0 0.0 copy-done.4
  94.0 0.0 copy-start.1
  94.0 0.6 copy.24
  94.6 0.6 copy.23
  95.2 0.0 copy-done.3
  95.3 0.7 copy.22
  96.0 0.7 copy.21
  96.8 0.0 copy-done.1
  96.8 1.0 %copy_bitcast_fusion = bf16[1,192,16,128]{3,2,1,0:T(8,128)(2,1)} fusion(bf16[2,1536,128]{2,1,0:T(8,128)(2,1)S(1)} %copy-done.1), kind=kLoop, calls=%fused_computation.2 | loop fusion | bytes 1572864 | tf_op jit(solution)/shard_map/reshape | solution.py:523
  (3 shorter events, 0.0 us)
Async XLA Ops:
  0.6 4.7 %copy-start = (bf16[1,192,16,128]{3,2,1,0:T(8,128)(2,1)S(1)}, bf16[1,192,16,128]{3,2,1,0:T(8,128)(2,1)}, u32[]{:S(2)}) copy-start(bf16[1,192,16,128]{3,2,1,0:T(8,128)(2,1)} %param.7) | copy-start | bytes 2359300
  0.6 4.7 %copy-start.2 = (bf16[1,192,16,128]{3,2,1,0:T(8,128)(2,1)S(1)}, bf16[1,192,16,128]{3,2,1,0:T(8,128)(2,1)}, u32[]{:S(2)}) copy-start(bf16[1,192,16,128]{3,2,1,0:T(8,128)(2,1)} %param.12) | copy-start | bytes 2359300
  91.7 2.3 %copy-start.4 = (bf16[2,2,32,128]{3,2,1,0:T(8,128)(2,1)S(1)}, bf16[2,2,32,128]{3,2,1,0:T(8,128)(2,1)}, u32[]{:S(2)}) copy-start(bf16[2,2,32,128]{3,2,1,0:T(8,128)(2,1)} %get-tuple-element.13) | copy-start | bytes 98308
  91.7 3.6 %copy-start.3 = (bf16[2,2,192,128]{3,2,1,0:T(8,128)(2,1)S(1)}, bf16[2,2,192,128]{3,2,1,0:T(8,128)(2,1)}, u32[]{:S(2)}) copy-start(bf16[2,2,192,128]{3,2,1,0:T(8,128)(2,1)} %get-tuple-element.12) | copy-start | bytes 589828
  94.0 2.8 %copy-start.1 = (bf16[2,1536,128]{2,1,0:T(8,128)(2,1)S(1)}, bf16[2,1536,128]{2,1,0:T(8,128)(2,1)}, u32[]{:S(2)}) copy-start(bf16[2,1536,128]{2,1,0:T(8,128)(2,1)} %get-tuple-element.11) | copy-start | bytes 2359300

commit v4 on v3

--- a/solution.py
+++ b/solution.py
@@ -27,12 +27,59 @@
 TN = (((0,), (0,)), ((), ()))
 
 
+F_PROMPT, F_FULL, F_DIAG, F_END, B_PROMPT, B_FULL, B_DIAG = range(7)
+W_ROLL, W_Q, W_DO, W_TILE, SEND, PASS, ROLLS, PROMPT, DQ, GPY = (1 << i for i in range(10))
+
+
+def schedule(x):
+    low, top = min(x, 3 - x), max(x, 3 - x)
+    late = 1 if x < 2 else 0
+    steps = []
+
+    def forward(b, tiles, waits):
+        for t in tiles:
+            last = top if b == late else low
+            steps.append((F_DIAG if t == last else F_FULL, b, t, W_TILE if t in waits else 0))
+
+    def prompt(b):
+        steps.append((F_PROMPT, b, 0, W_Q if b else 0))
+        steps.append((F_PROMPT, b, 1, 0 if b else W_ROLL))
+
+    def backward_low(b):
+        steps.append((B_PROMPT, b, 0, 0))
+        for t in range(low + 1):
+            last = t == low
+            steps.append((B_DIAG if last else B_FULL, b, t, DQ if last else 0))
+
+    prompt(0)
+    if late:
+        forward(0, range(low + 1), range(low + 1))
+        steps.append((F_END, 0, 0, 0))
+        backward_low(0)
+        prompt(1)
+        forward(1, range(top + 1), range(low + 1, top + 1))
+        steps.append((F_END, 1, 0, W_DO))
+    else:
+        forward(0, (0, 1), (0, 1))
+        prompt(1)
+        forward(0, range(2, top + 1), range(2, top + 1))
+        steps.append((F_END, 0, 0, 0))
+        forward(1, range(low + 1), ())
+        steps.append((F_END, 1, 0, W_DO))
+        backward_low(1)
+    steps.append((B_PROMPT, late, 0, GPY))
+    for i, t in enumerate(range(top, -1, -1)):
+        flags = SEND | (ROLLS if i == 0 else PASS) | (PROMPT if i == 1 else 0) | (DQ if t == 0 else 0)
+        steps.append((B_DIAG if t == top else B_FULL, late, t, flags))
+    return [kind + 8 * b + 16 * t + 64 * flags for kind, b, t, flags in steps]
+
+
 def dot(a, b, dims=NN):
     return lax.dot_general(a, b, dims, preferred_element_type=f32)
 
 
 def kernel(
-    q_in, do_in, kv_in, pk_in,
+    length, q_in, do_in, kvp_in,
     out, dq, dkv_out, dp_out,
     q2, do2, kv, acc, mx, tot, lse, off, o16, dk, dv, g16,
     zr, yrp, gyp, zrp, gx, gxp, xr, xrp,
@@ -42,6 +89,8 @@
     s = lax.axis_index("seq")
     r = lax.axis_index("roll")
     x, z = s // 4, s % 4
+    kv_in = kvp_in.at[:, :, pl.ds(0, BLK), :]
+    pk_in = kvp_in.at[:, :, pl.ds(BLK, 32), :]
     hs = x // 2
     top = jnp.maximum(x, 3 - x)
     partner = 4 * (3 - x) + z
@@ -113,6 +162,8 @@
     acc[...] = jnp.zeros_like(acc)
     mx[...] = jnp.full_like(mx, NEG)
     tot[...] = jnp.zeros_like(tot)
+    dk[...] = jnp.zeros_like(dk)
+    dv[...] = jnp.zeros_like(dv)
     own_p.wait()
 
     @pl.loop(1, 4)
@@ -168,6 +219,7 @@
         acc[b] = acc[b] * shrink + dot(kv[1, rows, :], lifted.astype(bf16), TN)
 
     own_q.wait()
+    own_do.wait()
 
     def wait_tile(tile):
         @pl.loop(1, 4)
@@ -175,63 +227,6 @@
             zz = (z + d) % 4
             rows = kv_rows(4 * tile + zz)
             remote(rows, rows, kvzs.at[zz, tile], kvzr.at[zz, tile], seq=4 * x + zz).wait_recv()
-
-    @pl.loop(0, 2)
-    def _(b):
-        blk = block_of(b)
-        last = blk // 4
-
-        @pl.when(b == 1)
-        def _():
-            q_out.wait_recv()
-
-        @pl.loop(0, 2)
-        def _(i):
-            half = (r + i) % 2
-
-            @pl.when((b == 0) & (i == 1))
-            def _():
-                @pl.loop(0, 4)
-                def _(zz):
-                    remote(p_column(half, zz), p_column(half, zz), ppys.at[zz], ppyr.at[zz], roll=half).wait_recv()
-
-            forward_tile(b, half * 512, 512, False)
-
-        @pl.loop(0, last)
-        def _(tile):
-            @pl.when((b == 0) | (tile > x))
-            def _():
-                wait_tile(tile)
-
-            forward_tile(b, PRM + tile * TILE, TILE, False)
-
-        @pl.when((b == 0) | (last > x))
-        def _():
-            wait_tile(last)
-
-        @pl.loop(0, 1 + z // 2)
-        def _(half):
-            forward_tile(b, PRM + last * TILE + half * HALF, HALF, True)
-
-    own_do.wait()
-    do_out.wait_recv()
-
-    @pl.loop(0, 2)
-    def _(b):
-        total = tot[b]
-        normal = acc[b] / total
-        lse[b] = mx[b] + jnp.log2(total)
-        off[b] = jnp.sum(normal * do2[b].astype(f32).T, 0, keepdims=True)
-        o16[b] = normal.T.astype(bf16)
-
-    own_out = pltpu.make_async_copy(o16.at[0], out.at[hs], lsem.at[4])
-    own_out.start()
-    out_out = remote(o16.at[1], out.at[hs], osem.at[0], osem.at[1], seq=partner)
-    out_out.start()
-
-    acc[...] = jnp.zeros_like(acc)
-    dk[...] = jnp.zeros_like(dk)
-    dv[...] = jnp.zeros_like(dv)
 
     def backward_tile(b, k0, size, masked):
         rows = pl.ds(pl.multiple_of(k0, 64), size)
@@ -326,72 +321,124 @@
 
     dq_out = remote(o16.at[3], dq.at[hs], osem.at[2], osem.at[3], seq=partner)
 
-    low = jnp.minimum(x, 3 - x)
-    early = 3 - 2 * low
-    later = jnp.where(x < 2, 1, 0)
-
-    @pl.loop(0, 7)
+    own_out = pltpu.make_async_copy(o16.at[0], out.at[hs], lsem.at[4])
+    out_out = remote(o16.at[1], out.at[hs], osem.at[0], osem.at[1], seq=partner)
+    own_dq = pltpu.make_async_copy(o16.at[2], dq.at[hs], lsem.at[7])
+    plans = [schedule(xx) for xx in range(4)]
+
+    @pl.loop(0, len(plans[0]))
     def _(i):
-        k = i - early - 2
-        rest = k >= 0
-        first = i < early
-        prompt = (i >= early) & (k < 0)
-        second = k > low
-        b = jnp.where(first, later, jnp.where(prompt, early + 1 - i, jnp.where(second, 0, 1)))
-        tile = jnp.where(first, 3 - low - i, jnp.where(second, k - low - 1, jnp.maximum(k, 0)))
-        diagonal = (i == 0) | (rest & (b != later) & (tile == low))
-
-        @pl.when(prompt)
+        code = jnp.int32(0)
+        for n, column in enumerate(zip(*plans)):
+            here = jnp.where(x == 0, column[0], jnp.where(x == 1, column[1], jnp.where(x == 2, column[2], column[3])))
+            code = jnp.where(i == n, here, code)
+        kind = code % 8
+        b = code // 8 % 2
+        tile = code // 16 % 4
+        flags = code // 64
+
+        def has(flag):
+            return flags // flag % 2 == 1
+
+        @pl.when(has(W_Q))
+        def _():
+            q_out.wait_recv()
+
+        @pl.when(has(W_ROLL))
+        def _():
+            @pl.loop(0, 4)
+            def _(zz):
+                rows = p_column(1 - r, zz)
+                remote(rows, rows, ppys.at[zz], ppyr.at[zz], roll=1 - r).wait_recv()
+
+        @pl.when(has(W_TILE))
+        def _():
+            wait_tile(tile)
+
+        @pl.when(has(W_DO))
+        def _():
+            do_out.wait_recv()
+
+        @pl.when(kind == F_PROMPT)
+        def _():
+            forward_tile(b, (r + tile) % 2 * 512, 512, False)
+
+        @pl.when(kind == F_FULL)
+        def _():
+            forward_tile(b, PRM + tile * TILE, TILE, False)
+
+        @pl.when(kind == F_DIAG)
+        def _():
+            @pl.loop(0, 1 + z // 2)
+            def _(half):
+                forward_tile(b, PRM + tile * TILE + half * HALF, HALF, True)
+
+        @pl.when(kind == F_END)
+        def _():
+            total = tot[b]
+            normal = acc[b] / total
+            lse[b] = mx[b] + jnp.log2(total)
+            off[b] = jnp.sum(normal * do2[b].astype(f32).T, 0, keepdims=True)
+            row_pos = block_of(b) * BLK + lax.broadcasted_iota(jnp.int32, (1, RB), 1) // PG
+            o16[b] = jnp.where(row_pos < length[0], normal, 0.0).T.astype(bf16)
+            acc[b] = jnp.zeros(acc.shape[1:], f32)
+
+            @pl.when(b == 0)
+            def _():
+                own_out.start()
+
+            @pl.when(b == 1)
+            def _():
+                out_out.start()
+
+        @pl.when(kind == B_PROMPT)
         def _():
             backward_tile(b, 0, PRM, False)
 
-        @pl.when((first | rest) & jnp.logical_not(diagonal))
+        @pl.when(kind == B_FULL)
         def _():
             backward_tile(b, PRM + tile * TILE, TILE, False)
 
-        @pl.when(diagonal)
+        @pl.when(kind == B_DIAG)
         def _():
             @pl.loop(0, 1 + z // 2)
             def _(half):
                 backward_tile(b, PRM + tile * TILE + half * HALF, HALF, True)
 
-        @pl.when(first | (rest & second))
+        @pl.when(has(SEND))
         def _():
             send_tile(tile)
 
-        @pl.when((i > 0) & (i <= early))
-        def _():
-            pass_tile(4 - low - i)
-
-        @pl.when(i == early + 1)
+        @pl.when(has(GPY))
         def _():
             finish_rows(0, PRM)
             gpy_out.start()
 
-        @pl.when(k == 0)
+        @pl.when(has(DQ))
+        def _():
+            o16[2 + b] = (acc[b] * SCALE).T.astype(bf16)
+
+            @pl.when(b == 0)
+            def _():
+                own_dq.start()
+
+            @pl.when(b == 1)
+            def _():
+                dq_out.start()
+
+        @pl.when(has(ROLLS))
         def _():
             pass_rolls()
 
-        @pl.when(k == 1)
+        @pl.when(has(PASS))
+        def _():
+            pass_tile(tile + 1)
+
+        @pl.when(has(PROMPT))
         def _():
             pass_prompt()
 
-        @pl.when(k == low)
-        def _():
-            o16[3] = (acc[1] * SCALE).T.astype(bf16)
-            dq_out.start()
-
-        @pl.when(k == 2 * low + 1)
-        def _():
-            o16[2] = (acc[0] * SCALE).T.astype(bf16)
-
-            @pl.when(low == 1)
-            def _():
-                pass_tile(0)
-
-    own_dq = pltpu.make_async_copy(o16.at[2], dq.at[hs], lsem.at[7])
-    own_dq.start()
-    pass_tile(low)
+    pass_tile(0)
 
     @pl.loop(1, 4)
     def _(d):
@@ -448,7 +495,7 @@
             gz_copy(zz, tile).wait_send()
 
 
-def attention(q_rows, do_rows, kv_rows, prompt_rows):
+def attention(lengths, q_rows, do_rows, kvp_rows):
     any_spec = pl.BlockSpec(memory_space=pl.ANY)
     vmem = pl.BlockSpec(memory_space=pltpu.VMEM)
     dma = pltpu.SemaphoreType.DMA
@@ -460,7 +507,7 @@
             jax.ShapeDtypeStruct((2, 2, BLK, HD), bf16),
             jax.ShapeDtypeStruct((2, 2, 32, HD), bf16),
         ],
-        in_specs=[any_spec] * 4,
+        in_specs=[pl.BlockSpec(memory_space=pltpu.SMEM)] + [any_spec] * 3,
         out_specs=[any_spec, any_spec, vmem, vmem],
         scratch_shapes=[
             pltpu.VMEM((2, RB, HD), bf16),
@@ -509,7 +556,7 @@
         compiler_params=pltpu.CompilerParams(
             collective_id=0, has_side_effects=True, vmem_limit_bytes=58 * 2**20
         ),
-    )(q_rows, do_rows, kv_rows, prompt_rows)
+    )(lengths, q_rows, do_rows, kvp_rows)
 
 
 def local(queries, rollout_keys, rollout_values, prompt_keys, prompt_values, grad_out, lengths):
@@ -525,11 +572,10 @@
     q_rows = by_group(queries[0]).reshape(2, RB, HD)
     cot = by_group(grad_out[0])
     do_rows = jnp.where(valid, cot, jnp.zeros_like(cot)).reshape(2, RB, HD)
-    kv_rows = jnp.stack([rollout_keys[0], rollout_values[0]]).transpose(2, 0, 1, 3)
-    prompt_rows = jnp.stack([prompt_keys, prompt_values]).transpose(2, 0, 1, 3)
-    out, dq, dkv, dprompt = attention(q_rows, do_rows, kv_rows, prompt_rows)
+    joined = jnp.concatenate([rollout_keys[0], prompt_keys, rollout_values[0], prompt_values])
+    joined = lax.optimization_barrier(joined).reshape(2, BLK + 32, 2, HD)
+    out, dq, dkv, dprompt = attention(lengths, q_rows, do_rows, joined.transpose(2, 0, 1, 3))
     out = out.reshape(2, BLK, PG, HD)
-    out = jnp.where(valid, out, jnp.zeros_like(out))
     dkv = dkv.transpose(1, 2, 0, 3)
     dprompt = dprompt.transpose(1, 2, 0, 3)
     return (

time: 98 us -> 93.3 us (0.952)
  Pallas kernels: 84.8 us -> 82.1 us
  other arithmetic: 5.17 us -> 2.85 us
    pallas_call x1, Pallas kernels: 84.8 us -> 82.1 us  [attention(): pl.pallas_call(kernel, out_shape=[jax.ShapeDtypeStruct((2, RB, HD), bf16)...]
    reshape x1 -> x0, other arithmetic: 2.33 us -> none  [merged(): return rows.transpose(1, 0, 2, 3).reshape(1, BLK, 2 * PG, HD)]
    reshape x1 -> x2, local copies, waits for them, and re-layouts: 1.01 us -> 3.2 us  [merged(): return rows.transpose(1, 0, 2, 3).reshape(1, BLK, 2 * PG, HD)]
    unnamed x16 -> x14, local copies, waits for them, and re-layouts: 4.56 us -> 2.75 us
    concatenate x0 -> x1, other arithmetic: none -> 1.32 us  [local(): jnp.concatenate([rollout_keys[0], prompt_keys, rollout_values[0], prompt_...]
    transpose x2 -> x0, other arithmetic: 1.31 us -> none  [the longest x1 0.69 us: local(): jnp.stack([rollout_keys[0], rollout_values[0]]).transpose(2, 0, 1, 3)]
where the time goes in v4:
time: 93.3 us; the launch traced here: 93.1 us
  Pallas kernels  82.1 us (88%)
  local copies, waits for them, and re-layouts  6.68 us (7%)
  other arithmetic  2.85 us (3%)
  between operations  1.46 us (2%)
    pallas_call x1, Pallas kernels, attention(): pl.pallas_call(kernel, out_shape=[jax.ShapeDtypeStruct((2, RB, HD), bf16)...  82.1 us
    reshape x2, local copies, waits for them, and re-layouts, merged(): return rows.transpose(1, 0, 2, 3).reshape(1, BLK, 2 * PG, HD)  3.2 us
    unnamed x14, local copies, waits for them, and re-layouts  2.75 us

profile of v4, /device:TPU:0, one launch (start us, length us, event | category | flops | bytes accessed | tf_op | source)
XLA Modules:
  0.0 93.1 jit_solution(8681003459832855773)
XLA Ops:
  0.6 0.0 copy-start
  0.6 0.0 copy-start.2
  1.4 1.3 %pad_maximum_fusion = bf16[448,2,128]{2,1,0:T(2,128)(2,1)S(1)} fusion(bf16[32,2,128]{2,1,0:T(2,128)(2,1)} %param.11, bf16[192,2,128]{2,1,0:T(2,128)(2,1)} %bitcast.43, bf16[32,2,128]{2,1,0:T(2,128)(2,1)} %param.10, bf16[192,2,128]{2,1,0:T(2,128)(2,1)} %bitcast.44), kind=kLoop, calls=%fused_computation.5 | loop fusion | flops 344064 | bytes 458752 | tf_op jit(solution)/shard_map/concatenate | solution.py:575
  2.8 0.7 copy.15
  3.5 0.0 copy-done
  3.5 0.0 copy-done.2
  3.5 1.5 %fusion = (bf16[2,1536,128]{2,1,0:T(8,128)(2,1)}, bf16[2,1536,128]{2,1,0:T(8,128)(2,1)}) fusion(pred[192]{0:T(512)(128)(4,1)S(1)} %add_compare_fusion, bf16[1,192,16,128]{3,2,1,0:T(8,128)(2,1)S(1)} %copy-done, bf16[1,192,16,128]{3,2,1,0:T(8,128)(2,1)S(1)} %copy-done.2), kind=kLoop, calls=%fused_computation.3 | loop fusion | flops 393216 | bytes 3145920 | tf_op jit(solution)/shard_map/reshape | solution.py:574
  5.0 82.1 %shard_map.118 = (bf16[2,1536,128]{2,1,0:T(8,128)(2,1)}, bf16[2,1536,128]{2,1,0:T(8,128)(2,1)}, bf16[2,2,192,128]{3,2,1,0:T(8,128)(2,1)}, bf16[2,2,32,128]{3,2,1,0:T(8,128)(2,1)}) custom-call(s32[1]{0:T(128)} %copy.28.length, bf16[2,1536,128]{2,1,0:T(8,128)(2,1)} %get-tuple-element.25.q_in, bf16[2,1536,128]{2,1,0:T(8,128)(2,1)} %get-tuple-element.24.do_in, ...), custom_call_target="tpu_custom_call" | custom-call | tf_op jit(solution)/shard_map/pallas_call | solution.py:502
  87.1 0.0 copy-start.4
  87.1 0.0 copy-start.3
  87.1 2.2 %copy_bitcast_fusion.1 = bf16[1,192,16,128]{3,2,1,0:T(8,128)(2,1)} fusion(bf16[2,1536,128]{2,1,0:T(8,128)(2,1)} %get-tuple-element.10), kind=kLoop, calls=%fused_computation.1 | loop fusion | bytes 1572864 | tf_op jit(solution)/shard_map/reshape | solution.py:570
  89.3 0.0 copy-done.4
  89.3 0.0 copy-start.1
  89.3 0.6 copy.21
  89.9 0.6 copy.20
  90.6 0.0 copy-done.3
  90.6 0.7 copy.19
  91.3 0.7 copy.18
  92.1 0.0 copy-done.1
  92.1 1.0 %copy_bitcast_fusion = bf16[1,192,16,128]{3,2,1,0:T(8,128)(2,1)} fusion(bf16[2,1536,128]{2,1,0:T(8,128)(2,1)S(1)} %copy-done.1), kind=kLoop, calls=%fused_computation | loop fusion | bytes 1572864 | tf_op jit(solution)/shard_map/reshape | solution.py:570
  (3 shorter events, 0.0 us)
Async XLA Ops:
  0.6 2.8 %copy-start = (bf16[1,192,16,128]{3,2,1,0:T(8,128)(2,1)S(1)}, bf16[1,192,16,128]{3,2,1,0:T(8,128)(2,1)}, u32[]{:S(2)}) copy-start(bf16[1,192,16,128]{3,2,1,0:T(8,128)(2,1)} %param.7) | copy-start | bytes 2359300
  0.6 2.8 %copy-start.2 = (bf16[1,192,16,128]{3,2,1,0:T(8,128)(2,1)S(1)}, bf16[1,192,16,128]{3,2,1,0:T(8,128)(2,1)}, u32[]{:S(2)}) copy-start(bf16[1,192,16,128]{3,2,1,0:T(8,128)(2,1)} %param.12) | copy-start | bytes 2359300
  87.1 2.2 %copy-start.4 = (bf16[2,2,32,128]{3,2,1,0:T(8,128)(2,1)S(1)}, bf16[2,2,32,128]{3,2,1,0:T(8,128)(2,1)}, u32[]{:S(2)}) copy-start(bf16[2,2,32,128]{3,2,1,0:T(8,128)(2,1)} %get-tuple-element.13) | copy-start | bytes 98308
  87.1 3.4 %copy-start.3 = (bf16[2,2,192,128]{3,2,1,0:T(8,128)(2,1)S(1)}, bf16[2,2,192,128]{3,2,1,0:T(8,128)(2,1)}, u32[]{:S(2)}) copy-start(bf16[2,2,192,128]{3,2,1,0:T(8,128)(2,1)} %get-tuple-element.12) | copy-start | bytes 589828
  89.3 2.8 %copy-start.1 = (bf16[2,1536,128]{2,1,0:T(8,128)(2,1)S(1)}, bf16[2,1536,128]{2,1,0:T(8,128)(2,1)}, u32[]{:S(2)}) copy-start(bf16[2,1536,128]{2,1,0:T(8,128)(2,1)} %get-tuple-element.11) | copy-start | bytes 2359300

commit v5 on v4

--- a/solution.py
+++ b/solution.py
@@ -28,7 +28,7 @@
 
 
 F_PROMPT, F_FULL, F_DIAG, F_END, B_PROMPT, B_FULL, B_DIAG = range(7)
-W_ROLL, W_Q, W_DO, W_TILE, SEND, PASS, ROLLS, PROMPT, DQ, GPY = (1 << i for i in range(10))
+W_ROLL, W_Q, W_DO, W_TILE, SEND, PASS, DQ, GPY = (1 << i for i in range(8))
 
 
 def schedule(x):
@@ -67,9 +67,10 @@
         forward(1, range(low + 1), ())
         steps.append((F_END, 1, 0, W_DO))
         backward_low(1)
-    steps.append((B_PROMPT, late, 0, GPY))
-    for i, t in enumerate(range(top, -1, -1)):
-        flags = SEND | (ROLLS if i == 0 else PASS) | (PROMPT if i == 1 else 0) | (DQ if t == 0 else 0)
+    for t in range(top, -1, -1):
+        if t == 0:
+            steps.append((B_PROMPT, late, 0, GPY | PASS))
+        flags = SEND | (PASS if 0 < t < top else 0) | (DQ if t == 0 else 0)
         steps.append((B_DIAG if t == top else B_FULL, late, t, flags))
     return [kind + 8 * b + 16 * t + 64 * flags for kind, b, t, flags in steps]
 
@@ -84,7 +85,7 @@
     q2, do2, kv, acc, mx, tot, lse, off, o16, dk, dv, g16,
     zr, yrp, gyp, zrp, gx, gxp, xr, xrp,
     lsem, kvxs, kvxr, kvzs, kvzr, ppxs, ppxr, ppzs, ppzr, ppys, ppyr, qsem, osem,
-    gzs, gzr, gpys, gpzs, gpzr, gxs, gxr, gpxs, gpxr,
+    dsem, gzs, gzr, gpys, gpzs, gpzr, gxs, gxr, gpxs, gpxr,
 ):
     s = lax.axis_index("seq")
     r = lax.axis_index("roll")
@@ -228,7 +229,7 @@
             rows = kv_rows(4 * tile + zz)
             remote(rows, rows, kvzs.at[zz, tile], kvzr.at[zz, tile], seq=4 * x + zz).wait_recv()
 
-    def backward_tile(b, k0, size, masked):
+    def backward_tile(b, k0, size, masked, after=lambda c: None):
         rows = pl.ds(pl.multiple_of(k0, 64), size)
 
         for c in range(RB // RC):
@@ -243,6 +244,7 @@
             dv[rows, :] += dot(weights.astype(bf16), cot)
             dk[rows, :] += dot(grads, queries)
             acc[b, :, part] += dot(keys, grads, TN)
+            after(c)
 
     def finish_rows(k0, size):
         rows = pl.ds(pl.multiple_of(k0, 64), size)
@@ -319,11 +321,27 @@
 
         xrp[x] = gxp[:, pl.ds(pl.multiple_of(x * 32, 32), 32), :]
 
-    dq_out = remote(o16.at[3], dq.at[hs], osem.at[2], osem.at[3], seq=partner)
+    def dq_copies(c):
+        rows = pl.ds(c * RC, RC)
+        return (
+            pltpu.make_async_copy(o16.at[2, rows, :], dq.at[hs, rows, :], dsem.at[c]),
+            remote(o16.at[3, rows, :], dq.at[hs, rows, :], dsem.at[2 + c], dsem.at[4 + c], seq=partner),
+        )
+
+    def send_dq(b, c):
+        rows = pl.ds(c * RC, RC)
+        o16[2 + b, rows, :] = (acc[b, :, rows] * SCALE).T.astype(bf16)
+
+        @pl.when(b == 0)
+        def _():
+            dq_copies(c)[0].start()
+
+        @pl.when(b == 1)
+        def _():
+            dq_copies(c)[1].start()
 
     own_out = pltpu.make_async_copy(o16.at[0], out.at[hs], lsem.at[4])
     out_out = remote(o16.at[1], out.at[hs], osem.at[0], osem.at[1], seq=partner)
-    own_dq = pltpu.make_async_copy(o16.at[2], dq.at[hs], lsem.at[7])
     plans = [schedule(xx) for xx in range(4)]
 
     @pl.loop(0, len(plans[0]))
@@ -397,7 +415,12 @@
 
         @pl.when(kind == B_FULL)
         def _():
-            backward_tile(b, PRM + tile * TILE, TILE, False)
+            def after(c):
+                @pl.when(has(DQ))
+                def _():
+                    send_dq(b, c)
+
+            backward_tile(b, PRM + tile * TILE, TILE, False, after)
 
         @pl.when(kind == B_DIAG)
         def _():
@@ -405,6 +428,11 @@
             def _(half):
                 backward_tile(b, PRM + tile * TILE + half * HALF, HALF, True)
 
+            @pl.when(has(DQ))
+            def _():
+                for c in range(RB // RC):
+                    send_dq(b, c)
+
         @pl.when(has(SEND))
         def _():
             send_tile(tile)
@@ -414,31 +442,13 @@
             finish_rows(0, PRM)
             gpy_out.start()
 
-        @pl.when(has(DQ))
-        def _():
-            o16[2 + b] = (acc[b] * SCALE).T.astype(bf16)
-
-            @pl.when(b == 0)
-            def _():
-                own_dq.start()
-
-            @pl.when(b == 1)
-            def _():
-                dq_out.start()
-
-        @pl.when(has(ROLLS))
-        def _():
-            pass_rolls()
-
         @pl.when(has(PASS))
         def _():
             pass_tile(tile + 1)
 
-        @pl.when(has(PROMPT))
-        def _():
-            pass_prompt()
-
+    pass_rolls()
     pass_tile(0)
+    pass_prompt()
 
     @pl.loop(1, 4)
     def _(d):
@@ -467,9 +477,10 @@
     q_out.wait_send()
     do_out.wait_send()
     out_out.wait()
-    dq_out.wait()
     own_out.wait()
-    own_dq.wait()
+    for c in range(RB // RC):
+        for copy in dq_copies(c):
+            copy.wait()
 
     @pl.loop(1, 4)
     def _(d):
@@ -542,7 +553,8 @@
             dma((4,)),
             dma((4,)),
             dma((4,)),
-            dma((4,)),
+            dma((2,)),
+            dma((6,)),
             dma((4, 4)),
             dma((4, 4)),
             dma((2,)),

time: 93.3 us -> 92.3 us (0.989)
  no operation moved by 1% of the time
where the time goes in v5:
time: 92.3 us; the launch traced here: 92.2 us
  Pallas kernels  81.2 us (88%)
  local copies, waits for them, and re-layouts  6.68 us (7%)
  other arithmetic  2.85 us (3%)
  between operations  1.46 us (2%)
    pallas_call x1, Pallas kernels, attention(): pl.pallas_call(kernel, out_shape=[jax.ShapeDtypeStruct((2, RB, HD), bf16)...  81.2 us
    reshape x2, local copies, waits for them, and re-layouts, merged(): return rows.transpose(1, 0, 2, 3).reshape(1, BLK, 2 * PG, HD)  3.2 us
    unnamed x14, local copies, waits for them, and re-layouts  2.75 us

profile of v5, /device:TPU:0, one launch (start us, length us, event | category | flops | bytes accessed | tf_op | source)
XLA Modules:
  0.0 92.2 jit_solution(5324101305495282841)
XLA Ops:
  0.6 0.0 copy-start
  0.6 0.0 copy-start.2
  1.4 1.3 %pad_maximum_fusion = bf16[448,2,128]{2,1,0:T(2,128)(2,1)S(1)} fusion(bf16[32,2,128]{2,1,0:T(2,128)(2,1)} %param.11, bf16[192,2,128]{2,1,0:T(2,128)(2,1)} %bitcast.43, bf16[32,2,128]{2,1,0:T(2,128)(2,1)} %param.10, bf16[192,2,128]{2,1,0:T(2,128)(2,1)} %bitcast.44), kind=kLoop, calls=%fused_computation.5 | loop fusion | flops 344064 | bytes 458752 | tf_op jit(solution)/shard_map/concatenate | solution.py:587
  2.8 0.7 copy.15
  3.5 0.0 copy-done
  3.5 0.0 copy-done.2
  3.5 1.5 %fusion = (bf16[2,1536,128]{2,1,0:T(8,128)(2,1)}, bf16[2,1536,128]{2,1,0:T(8,128)(2,1)}) fusion(pred[192]{0:T(512)(128)(4,1)S(1)} %add_compare_fusion, bf16[1,192,16,128]{3,2,1,0:T(8,128)(2,1)S(1)} %copy-done, bf16[1,192,16,128]{3,2,1,0:T(8,128)(2,1)S(1)} %copy-done.2), kind=kLoop, calls=%fused_computation.3 | loop fusion | flops 393216 | bytes 3145920 | tf_op jit(solution)/shard_map/reshape | solution.py:586
  5.0 81.2 %shard_map.118 = (bf16[2,1536,128]{2,1,0:T(8,128)(2,1)}, bf16[2,1536,128]{2,1,0:T(8,128)(2,1)}, bf16[2,2,192,128]{3,2,1,0:T(8,128)(2,1)}, bf16[2,2,32,128]{3,2,1,0:T(8,128)(2,1)}) custom-call(s32[1]{0:T(128)} %copy.28.length, bf16[2,1536,128]{2,1,0:T(8,128)(2,1)} %get-tuple-element.25.q_in, bf16[2,1536,128]{2,1,0:T(8,128)(2,1)} %get-tuple-element.24.do_in, ...), custom_call_target="tpu_custom_call" | custom-call | tf_op jit(solution)/shard_map/pallas_call | solution.py:513
  86.2 0.0 copy-start.4
  86.2 0.0 copy-start.3
  86.2 2.2 %copy_bitcast_fusion.1 = bf16[1,192,16,128]{3,2,1,0:T(8,128)(2,1)} fusion(bf16[2,1536,128]{2,1,0:T(8,128)(2,1)} %get-tuple-element.10), kind=kLoop, calls=%fused_computation.1 | loop fusion | bytes 1572864 | tf_op jit(solution)/shard_map/reshape | solution.py:582
  88.4 0.0 copy-done.4
  88.4 0.0 copy-start.1
  88.4 0.6 copy.21
  89.0 0.6 copy.20
  89.6 0.0 copy-done.3
  89.7 0.7 copy.19
  90.4 0.7 copy.18
  91.1 0.0 copy-done.1
  91.1 1.0 %copy_bitcast_fusion = bf16[1,192,16,128]{3,2,1,0:T(8,128)(2,1)} fusion(bf16[2,1536,128]{2,1,0:T(8,128)(2,1)S(1)} %copy-done.1), kind=kLoop, calls=%fused_computation | loop fusion | bytes 1572864 | tf_op jit(solution)/shard_map/reshape | solution.py:582
  (3 shorter events, 0.0 us)
Async XLA Ops:
  0.6 2.8 %copy-start = (bf16[1,192,16,128]{3,2,1,0:T(8,128)(2,1)S(1)}, bf16[1,192,16,128]{3,2,1,0:T(8,128)(2,1)}, u32[]{:S(2)}) copy-start(bf16[1,192,16,128]{3,2,1,0:T(8,128)(2,1)} %param.7) | copy-start | bytes 2359300
  0.6 2.8 %copy-start.2 = (bf16[1,192,16,128]{3,2,1,0:T(8,128)(2,1)S(1)}, bf16[1,192,16,128]{3,2,1,0:T(8,128)(2,1)}, u32[]{:S(2)}) copy-start(bf16[1,192,16,128]{3,2,1,0:T(8,128)(2,1)} %param.12) | copy-start | bytes 2359300
  86.2 2.2 %copy-start.4 = (bf16[2,2,32,128]{3,2,1,0:T(8,128)(2,1)S(1)}, bf16[2,2,32,128]{3,2,1,0:T(8,128)(2,1)}, u32[]{:S(2)}) copy-start(bf16[2,2,32,128]{3,2,1,0:T(8,128)(2,1)} %get-tuple-element.13) | copy-start | bytes 98308
  86.2 3.4 %copy-start.3 = (bf16[2,2,192,128]{3,2,1,0:T(8,128)(2,1)S(1)}, bf16[2,2,192,128]{3,2,1,0:T(8,128)(2,1)}, u32[]{:S(2)}) copy-start(bf16[2,2,192,128]{3,2,1,0:T(8,128)(2,1)} %get-tuple-element.12) | copy-start | bytes 589828
  88.4 2.8 %copy-start.1 = (bf16[2,1536,128]{2,1,0:T(8,128)(2,1)S(1)}, bf16[2,1536,128]{2,1,0:T(8,128)(2,1)}, u32[]{:S(2)}) copy-start(bf16[2,1536,128]{2,1,0:T(8,128)(2,1)} %get-tuple-element.11) | copy-start | bytes 2359300

commit v6 on v5

--- a/solution.py
+++ b/solution.py
@@ -28,7 +28,7 @@
 
 
 F_PROMPT, F_FULL, F_DIAG, F_END, B_PROMPT, B_FULL, B_DIAG = range(7)
-W_ROLL, W_Q, W_DO, W_TILE, SEND, PASS, DQ, GPY = (1 << i for i in range(8))
+W_ROLL, W_Q, W_DO, W_TILE, SEND, DQ, GPY, PASS = (1 << i for i in range(8))
 
 
 def schedule(x):
@@ -67,11 +67,16 @@
         forward(1, range(low + 1), ())
         steps.append((F_END, 1, 0, W_DO))
         backward_low(1)
-    for t in range(top, -1, -1):
-        if t == 0:
-            steps.append((B_PROMPT, late, 0, GPY | PASS))
-        flags = SEND | (PASS if 0 < t < top else 0) | (DQ if t == 0 else 0)
+    order = [t for t in range(top, -1, -1) if t != x] + [x]
+    prompt_at = len(order) - (1 if x < 2 else 2)
+    sent = None
+    for i, t in enumerate(order):
+        if i == prompt_at:
+            steps.append((B_PROMPT, late, 0, GPY | PASS * (1 + sent)))
+            sent = None
+        flags = SEND | (0 if sent is None else PASS * (1 + sent)) | (DQ if i == len(order) - 1 else 0)
         steps.append((B_DIAG if t == top else B_FULL, late, t, flags))
+        sent = t
     return [kind + 8 * b + 16 * t + 64 * flags for kind, b, t, flags in steps]
 
 
@@ -143,6 +148,12 @@
         rows = kv_rows(4 * tile + z)
         return remote(rows, rows, kvzs.at[zz, tile], kvzr.at[z, tile], seq=4 * x + zz)
 
+    def uses(zz, tile, other):
+        return (tile != top) | (other <= zz // 2 * 2 + 1)
+
+    def gives(zz, tile, other):
+        return (tile != top) | (other < zz)
+
     def sees(xx):
         return x <= jnp.maximum(xx, 3 - xx)
 
@@ -187,7 +198,9 @@
 
         @pl.loop(1, 4)
         def _(d):
-            kvz_copy((z + d) % 4, tile).start()
+            @pl.when(uses((z + d) % 4, tile, z))
+            def _():
+                kvz_copy((z + d) % 4, tile).start()
 
     @pl.loop(1, 4)
     def _(d):
@@ -227,7 +240,10 @@
         def _(d):
             zz = (z + d) % 4
             rows = kv_rows(4 * tile + zz)
-            remote(rows, rows, kvzs.at[zz, tile], kvzr.at[zz, tile], seq=4 * x + zz).wait_recv()
+
+            @pl.when(uses(z, tile, zz))
+            def _():
+                remote(rows, rows, kvzs.at[zz, tile], kvzr.at[zz, tile], seq=4 * x + zz).wait_recv()
 
     def backward_tile(b, k0, size, masked, after=lambda c: None):
         rows = pl.ds(pl.multiple_of(k0, 64), size)
@@ -266,15 +282,22 @@
 
         @pl.loop(1, 4)
         def _(d):
-            gz_copy((z + d) % 4, tile).start()
+            @pl.when(gives(z, tile, (z + d) % 4))
+            def _():
+                gz_copy((z + d) % 4, tile).start()
 
     def pass_tile(tile):
         rows = grad_rows(4 * tile + z)
         total = g16[:, rows, :].astype(f32)
         for d in range(1, 4):
             zz = (z + d) % 4
-            remote(g16.at[:, rows, :], zr.at[zz, tile], gzs.at[zz, tile], gzr.at[zz, tile], seq=4 * x + zz).wait_recv()
-            total = total + zr[zz, tile].astype(f32)
+            given = gives(zz, tile, z)
+
+            @pl.when(given)
+            def _():
+                remote(g16.at[:, rows, :], zr.at[zz, tile], gzs.at[zz, tile], gzr.at[zz, tile], seq=4 * x + zz).wait_recv()
+
+            total = total + jnp.where(given, zr[zz, tile].astype(f32), 0.0)
 
         @pl.when(tile == x)
         def _():
@@ -442,12 +465,12 @@
             finish_rows(0, PRM)
             gpy_out.start()
 
-        @pl.when(has(PASS))
-        def _():
-            pass_tile(tile + 1)
+        @pl.when(flags >= PASS)
+        def _():
+            pass_tile(flags // PASS - 1)
 
     pass_rolls()
-    pass_tile(0)
+    pass_tile(x)
     pass_prompt()
 
     @pl.loop(1, 4)
@@ -502,8 +525,13 @@
 
         @pl.loop(0, top + 1)
         def _(tile):
-            kvz_copy(zz, tile).wait_send()
-            gz_copy(zz, tile).wait_send()
+            @pl.when(uses(zz, tile, z))
+            def _():
+                kvz_copy(zz, tile).wait_send()
+
+            @pl.when(gives(z, tile, zz))
+            def _():
+                gz_copy(zz, tile).wait_send()
 
 
 def attention(lengths, q_rows, do_rows, kvp_rows):

time: 92.3 us -> 92.3 us (level)
  no operation moved by 1% of the time
where the time goes in v6:
time: 92.3 us; the launch traced here: 92.1 us
  Pallas kernels  81.1 us (88%)
  local copies, waits for them, and re-layouts  6.68 us (7%)
  other arithmetic  2.85 us (3%)
  between operations  1.46 us (2%)
    pallas_call x1, Pallas kernels, attention(): pl.pallas_call(kernel, out_shape=[jax.ShapeDtypeStruct((2, RB, HD), bf16)...  81.1 us
    reshape x2, local copies, waits for them, and re-layouts, merged(): return rows.transpose(1, 0, 2, 3).reshape(1, BLK, 2 * PG, HD)  3.2 us
    unnamed x14, local copies, waits for them, and re-layouts  2.75 us

profile of v6, /device:TPU:0, one launch (start us, length us, event | category | flops | bytes accessed | tf_op | source)
XLA Modules:
  0.0 92.1 jit_solution(324413603520825365)
XLA Ops:
  0.6 0.0 copy-start
  0.6 0.0 copy-start.2
  1.4 1.3 %pad_maximum_fusion = bf16[448,2,128]{2,1,0:T(2,128)(2,1)S(1)} fusion(bf16[32,2,128]{2,1,0:T(2,128)(2,1)} %param.11, bf16[192,2,128]{2,1,0:T(2,128)(2,1)} %bitcast.43, bf16[32,2,128]{2,1,0:T(2,128)(2,1)} %param.10, bf16[192,2,128]{2,1,0:T(2,128)(2,1)} %bitcast.44), kind=kLoop, calls=%fused_computation.5 | loop fusion | flops 344064 | bytes 458752 | tf_op jit(solution)/shard_map/concatenate | solution.py:615
  2.8 0.7 copy.15
  3.5 0.0 copy-done
  3.5 0.0 copy-done.2
  3.5 1.5 %fusion = (bf16[2,1536,128]{2,1,0:T(8,128)(2,1)}, bf16[2,1536,128]{2,1,0:T(8,128)(2,1)}) fusion(pred[192]{0:T(512)(128)(4,1)S(1)} %add_compare_fusion, bf16[1,192,16,128]{3,2,1,0:T(8,128)(2,1)S(1)} %copy-done, bf16[1,192,16,128]{3,2,1,0:T(8,128)(2,1)S(1)} %copy-done.2), kind=kLoop, calls=%fused_computation.3 | loop fusion | flops 393216 | bytes 3145920 | tf_op jit(solution)/shard_map/reshape | solution.py:614
  5.0 81.1 %shard_map.118 = (bf16[2,1536,128]{2,1,0:T(8,128)(2,1)}, bf16[2,1536,128]{2,1,0:T(8,128)(2,1)}, bf16[2,2,192,128]{3,2,1,0:T(8,128)(2,1)}, bf16[2,2,32,128]{3,2,1,0:T(8,128)(2,1)}) custom-call(s32[1]{0:T(128)} %copy.28.length, bf16[2,1536,128]{2,1,0:T(8,128)(2,1)} %get-tuple-element.25.q_in, bf16[2,1536,128]{2,1,0:T(8,128)(2,1)} %get-tuple-element.24.do_in, ...), custom_call_target="tpu_custom_call" | custom-call | tf_op jit(solution)/shard_map/pallas_call | solution.py:541
  86.2 0.0 copy-start.4
  86.2 0.0 copy-start.3
  86.2 2.2 %copy_bitcast_fusion.1 = bf16[1,192,16,128]{3,2,1,0:T(8,128)(2,1)} fusion(bf16[2,1536,128]{2,1,0:T(8,128)(2,1)} %get-tuple-element.10), kind=kLoop, calls=%fused_computation.1 | loop fusion | bytes 1572864 | tf_op jit(solution)/shard_map/reshape | solution.py:610
  88.4 0.0 copy-done.4
  88.4 0.0 copy-start.1
  88.4 0.6 copy.21
  89.0 0.6 copy.20
  89.6 0.0 copy-done.3
  89.6 0.7 copy.19
  90.4 0.7 copy.18
  91.1 0.0 copy-done.1
  91.1 1.0 %copy_bitcast_fusion = bf16[1,192,16,128]{3,2,1,0:T(8,128)(2,1)} fusion(bf16[2,1536,128]{2,1,0:T(8,128)(2,1)S(1)} %copy-done.1), kind=kLoop, calls=%fused_computation | loop fusion | bytes 1572864 | tf_op jit(solution)/shard_map/reshape | solution.py:610
  (3 shorter events, 0.0 us)
Async XLA Ops:
  0.6 2.8 %copy-start = (bf16[1,192,16,128]{3,2,1,0:T(8,128)(2,1)S(1)}, bf16[1,192,16,128]{3,2,1,0:T(8,128)(2,1)}, u32[]{:S(2)}) copy-start(bf16[1,192,16,128]{3,2,1,0:T(8,128)(2,1)} %param.7) | copy-start | bytes 2359300
  0.6 2.8 %copy-start.2 = (bf16[1,192,16,128]{3,2,1,0:T(8,128)(2,1)S(1)}, bf16[1,192,16,128]{3,2,1,0:T(8,128)(2,1)}, u32[]{:S(2)}) copy-start(bf16[1,192,16,128]{3,2,1,0:T(8,128)(2,1)} %param.12) | copy-start | bytes 2359300
  86.2 2.2 %copy-start.4 = (bf16[2,2,32,128]{3,2,1,0:T(8,128)(2,1)S(1)}, bf16[2,2,32,128]{3,2,1,0:T(8,128)(2,1)}, u32[]{:S(2)}) copy-start(bf16[2,2,32,128]{3,2,1,0:T(8,128)(2,1)} %get-tuple-element.13) | copy-start | bytes 98308
  86.2 3.4 %copy-start.3 = (bf16[2,2,192,128]{3,2,1,0:T(8,128)(2,1)S(1)}, bf16[2,2,192,128]{3,2,1,0:T(8,128)(2,1)}, u32[]{:S(2)}) copy-start(bf16[2,2,192,128]{3,2,1,0:T(8,128)(2,1)} %get-tuple-element.12) | copy-start | bytes 589828
  88.4 2.8 %copy-start.1 = (bf16[2,1536,128]{2,1,0:T(8,128)(2,1)S(1)}, bf16[2,1536,128]{2,1,0:T(8,128)(2,1)}, u32[]{:S(2)}) copy-start(bf16[2,1536,128]{2,1,0:T(8,128)(2,1)} %get-tuple-element.11) | copy-start | bytes 2359300

commit v7 on v6

--- a/solution.py
+++ b/solution.py
@@ -69,14 +69,17 @@
         backward_low(1)
     order = [t for t in range(top, -1, -1) if t != x] + [x]
     prompt_at = len(order) - (1 if x < 2 else 2)
-    sent = None
+    waiting = []
     for i, t in enumerate(order):
         if i == prompt_at:
-            steps.append((B_PROMPT, late, 0, GPY | PASS * (1 + sent)))
-            sent = None
-        flags = SEND | (0 if sent is None else PASS * (1 + sent)) | (DQ if i == len(order) - 1 else 0)
+            ready = waiting.pop(0) if waiting and waiting[0][1] <= len(steps) - 2 else None
+            steps.append((B_PROMPT, late, 0, GPY + PASS * (0 if ready is None else 1 + ready[0])))
+        final = i == len(order) - 1
+        ready = waiting.pop(0) if waiting and (final or waiting[0][1] <= len(steps) - 2) else None
+        flags = SEND + PASS * (0 if ready is None else 1 + ready[0]) + (DQ if final else 0)
+        waiting.append((t, len(steps)))
         steps.append((B_DIAG if t == top else B_FULL, late, t, flags))
-        sent = t
+    assert [t for t, _ in waiting] == [x]
     return [kind + 8 * b + 16 * t + 64 * flags for kind, b, t, flags in steps]
 
 
@@ -87,7 +90,7 @@
 def kernel(
     length, q_in, do_in, kvp_in,
     out, dq, dkv_out, dp_out,
-    q2, do2, kv, acc, mx, tot, lse, off, o16, dk, dv, g16,
+    raw, q2, do2, kv, acc, mx, tot, lse, off, o16, dk, dv, g16,
     zr, yrp, gyp, zrp, gx, gxp, xr, xrp,
     lsem, kvxs, kvxr, kvzs, kvzr, ppxs, ppxr, ppzs, ppzr, ppys, ppyr, qsem, osem,
     dsem, gzs, gzr, gpys, gpzs, gpzr, gxs, gxr, gpxs, gpxr,
@@ -126,9 +129,9 @@
     own_p.start()
     own_kv = pltpu.make_async_copy(kv_in.at[hs], kv_rows(s), lsem.at[2])
     own_kv.start()
-    own_q = pltpu.make_async_copy(q_in.at[hs], q2.at[0], lsem.at[0])
+    own_q = pltpu.make_async_copy(q_in.at[:, hs], raw.at[0, 0], lsem.at[0])
     own_q.start()
-    own_do = pltpu.make_async_copy(do_in.at[hs], do2.at[0], lsem.at[1])
+    own_do = pltpu.make_async_copy(do_in.at[:, hs], raw.at[1, 0], lsem.at[1])
     own_do.start()
     pl.semaphore_wait(barrier, 7)
 
@@ -169,7 +172,7 @@
         def _():
             kvx_copy(xx).start()
 
-    q_out = remote(q_in.at[1 - hs], q2.at[1], qsem.at[0], qsem.at[1], seq=partner)
+    q_out = remote(q_in.at[:, 1 - hs], raw.at[0, 1], qsem.at[0], qsem.at[1], seq=partner)
     q_out.start()
     acc[...] = jnp.zeros_like(acc)
     mx[...] = jnp.full_like(mx, NEG)
@@ -208,7 +211,7 @@
         remote(p_column(r, zz), p_column(r, zz), ppzs.at[zz], ppzr.at[zz], seq=4 * x + zz).wait_recv()
         py_copy(zz).start()
 
-    do_out = remote(do_in.at[1 - hs], do2.at[1], qsem.at[2], qsem.at[3], seq=partner)
+    do_out = remote(do_in.at[:, 1 - hs], raw.at[1, 1], qsem.at[2], qsem.at[3], seq=partner)
     do_out.start()
 
     def block_of(b):
@@ -232,8 +235,18 @@
         tot[b] = tot[b] * shrink + jnp.sum(lifted, 0, keepdims=True)
         acc[b] = acc[b] * shrink + dot(kv[1, rows, :], lifted.astype(bf16), TN)
 
+    def take_q(b):
+        q2[b] = raw[0, b].reshape(RB, HD)
+
+    def take_do(b):
+        row_pos = block_of(b) * BLK + lax.broadcasted_iota(jnp.int32, (RB, HD), 0) // PG
+        rows = raw[1, b].reshape(RB, HD).astype(f32)
+        do2[b] = jnp.where(row_pos < length[0], rows, 0.0).astype(bf16)
+
     own_q.wait()
+    take_q(0)
     own_do.wait()
+    take_do(0)
 
     def wait_tile(tile):
         @pl.loop(1, 4)
@@ -345,15 +358,15 @@
         xrp[x] = gxp[:, pl.ds(pl.multiple_of(x * 32, 32), 32), :]
 
     def dq_copies(c):
-        rows = pl.ds(c * RC, RC)
+        rows = pl.ds(c * (RC // PG), RC // PG)
         return (
-            pltpu.make_async_copy(o16.at[2, rows, :], dq.at[hs, rows, :], dsem.at[c]),
-            remote(o16.at[3, rows, :], dq.at[hs, rows, :], dsem.at[2 + c], dsem.at[4 + c], seq=partner),
+            pltpu.make_async_copy(o16.at[2, rows], dq.at[rows, hs], dsem.at[c]),
+            remote(o16.at[3, rows], dq.at[rows, hs], dsem.at[2 + c], dsem.at[4 + c], seq=partner),
         )
 
     def send_dq(b, c):
-        rows = pl.ds(c * RC, RC)
-        o16[2 + b, rows, :] = (acc[b, :, rows] * SCALE).T.astype(bf16)
+        part = (acc[b, :, pl.ds(c * RC, RC)] * SCALE).T.astype(bf16)
+        o16[2 + b, pl.ds(c * (RC // PG), RC // PG)] = part.reshape(RC // PG, PG, HD)
 
         @pl.when(b == 0)
         def _():
@@ -363,8 +376,8 @@
         def _():
             dq_copies(c)[1].start()
 
-    own_out = pltpu.make_async_copy(o16.at[0], out.at[hs], lsem.at[4])
-    out_out = remote(o16.at[1], out.at[hs], osem.at[0], osem.at[1], seq=partner)
+    own_out = pltpu.make_async_copy(o16.at[0], out.at[:, hs], lsem.at[4])
+    out_out = remote(o16.at[1], out.at[:, hs], osem.at[0], osem.at[1], seq=partner)
     plans = [schedule(xx) for xx in range(4)]
 
     @pl.loop(0, len(plans[0]))
@@ -384,6 +397,7 @@
         @pl.when(has(W_Q))
         def _():
             q_out.wait_recv()
+            take_q(1)
 
         @pl.when(has(W_ROLL))
         def _():
@@ -399,6 +413,7 @@
         @pl.when(has(W_DO))
         def _():
             do_out.wait_recv()
+            take_do(1)
 
         @pl.when(kind == F_PROMPT)
         def _():
@@ -421,7 +436,7 @@
             lse[b] = mx[b] + jnp.log2(total)
             off[b] = jnp.sum(normal * do2[b].astype(f32).T, 0, keepdims=True)
             row_pos = block_of(b) * BLK + lax.broadcasted_iota(jnp.int32, (1, RB), 1) // PG
-            o16[b] = jnp.where(row_pos < length[0], normal, 0.0).T.astype(bf16)
+            o16[b] = jnp.where(row_pos < length[0], normal, 0.0).T.astype(bf16).reshape(BLK, PG, HD)
             acc[b] = jnp.zeros(acc.shape[1:], f32)
 
             @pl.when(b == 0)
@@ -541,14 +556,15 @@
     return pl.pallas_call(
         kernel,
         out_shape=[
-            jax.ShapeDtypeStruct((2, RB, HD), bf16),
-            jax.ShapeDtypeStruct((2, RB, HD), bf16),
+            jax.ShapeDtypeStruct((BLK, 2, PG, HD), bf16),
+            jax.ShapeDtypeStruct((BLK, 2, PG, HD), bf16),
             jax.ShapeDtypeStruct((2, 2, BLK, HD), bf16),
             jax.ShapeDtypeStruct((2, 2, 32, HD), bf16),
         ],
         in_specs=[pl.BlockSpec(memory_space=pltpu.SMEM)] + [any_spec] * 3,
         out_specs=[any_spec, any_spec, vmem, vmem],
         scratch_shapes=[
+            pltpu.VMEM((2, 2, BLK, PG, HD), bf16),
             pltpu.VMEM((2, RB, HD), bf16),
             pltpu.VMEM((2, RB, HD), bf16),
             pltpu.VMEM((2, PRM + N * BLK, HD), bf16),
@@ -557,7 +573,7 @@
             pltpu.VMEM((2, 1, RB), f32),
             pltpu.VMEM((2, 1, RB), f32),
             pltpu.VMEM((2, 1, RB), f32),
-            pltpu.VMEM((4, RB, HD), bf16),
+            pltpu.VMEM((4, BLK, PG, HD), bf16),
             pltpu.VMEM((PRM + N * BLK, HD), f32),
             pltpu.VMEM((PRM + N * BLK, HD), f32),
             pltpu.VMEM((2, PRM + N * BLK, HD), bf16),
@@ -600,27 +616,17 @@
 
 
 def local(queries, rollout_keys, rollout_values, prompt_keys, prompt_values, grad_out, lengths):
-    first_row = lax.axis_index("seq") * BLK
-    valid = ((first_row + jnp.arange(BLK, dtype=jnp.int32)) < lengths[0])[None, :, None, None]
-
-    def by_group(rows):
-        return rows.reshape(BLK, 2, PG, HD).transpose(1, 0, 2, 3)
-
-    def merged(rows):
-        return rows.transpose(1, 0, 2, 3).reshape(1, BLK, 2 * PG, HD)
-
-    q_rows = by_group(queries[0]).reshape(2, RB, HD)
-    cot = by_group(grad_out[0])
-    do_rows = jnp.where(valid, cot, jnp.zeros_like(cot)).reshape(2, RB, HD)
+    by_group = (BLK, 2, PG, HD)
+    q_rows = queries.reshape(by_group)
+    do_rows = grad_out.reshape(by_group)
     joined = jnp.concatenate([rollout_keys[0], prompt_keys, rollout_values[0], prompt_values])
     joined = lax.optimization_barrier(joined).reshape(2, BLK + 32, 2, HD)
     out, dq, dkv, dprompt = attention(lengths, q_rows, do_rows, joined.transpose(2, 0, 1, 3))
-    out = out.reshape(2, BLK, PG, HD)
     dkv = dkv.transpose(1, 2, 0, 3)
     dprompt = dprompt.transpose(1, 2, 0, 3)
     return (
-        merged(out),
-        merged(dq.reshape(2, BLK, PG, HD)),
+        out.reshape(queries.shape),
+        dq.reshape(queries.shape),
         dkv[0][None],
         dkv[1][None],
         dprompt[0],

time: 92.3 us -> 89.8 us (0.973)
  Pallas kernels: 81.1 us -> 79.4 us
  other arithmetic: 2.85 us -> 1.32 us
    reshape x2 -> x0, local copies, waits for them, and re-layouts: 3.2 us -> none  [merged(): return rows.transpose(1, 0, 2, 3).reshape(1, BLK, 2 * PG, HD)]
    unnamed x14 -> x10, local copies, waits for them, and re-layouts: 2.75 us -> 5.02 us
    pallas_call x1, Pallas kernels: 81.1 us -> 79.4 us  [attention(): pl.pallas_call(kernel, out_shape=[jax.ShapeDtypeStruct((BLK, 2, PG, HD),...]
    reshape x1 -> x0, other arithmetic: 1.52 us -> none  [local(): do_rows = jnp.where(valid, cot, jnp.zeros_like(cot)).reshape(2, RB, HD)]
    slice x1, local copies, waits for them, and re-layouts: 0.01 us -> 0.95 us  [local(): dkv[1][None]]
where the time goes in v7:
time: 89.8 us; the launch traced here: 89.6 us
  Pallas kernels  79.4 us (88%)
  local copies, waits for them, and re-layouts  7.51 us (8%)
  other arithmetic  1.32 us (1%)
  between operations  1.31 us (1%)
    pallas_call x1, Pallas kernels, attention(): pl.pallas_call(kernel, out_shape=[jax.ShapeDtypeStruct((BLK, 2, PG, HD),...  79.4 us
    unnamed x10, local copies, waits for them, and re-layouts  5.02 us

profile of v7, /device:TPU:0, one launch (start us, length us, event | category | flops | bytes accessed | tf_op | source)
XLA Modules:
  0.0 89.6 jit_solution(7967785111451563030)
XLA Ops:
  1.3 1.3 %pad_maximum_fusion = bf16[448,2,128]{2,1,0:T(2,128)(2,1)S(1)} fusion(bf16[32,2,128]{2,1,0:T(2,128)(2,1)} %param.11, bf16[192,2,128]{2,1,0:T(2,128)(2,1)} %bitcast.21, bf16[32,2,128]{2,1,0:T(2,128)(2,1)} %param.10, bf16[192,2,128]{2,1,0:T(2,128)(2,1)} %bitcast.22), kind=kLoop, calls=%fused_computation | loop fusion | flops 344064 | bytes 458752 | tf_op jit(solution)/shard_map/concatenate | solution.py:622
  2.6 0.7 copy.13
  3.3 79.4 %shard_map.118 = (bf16[192,2,8,128]{3,2,1,0:T(8,128)(2,1)}, bf16[192,2,8,128]{3,2,1,0:T(8,128)(2,1)}, bf16[2,2,192,128]{3,2,1,0:T(8,128)(2,1)}, bf16[2,2,32,128]{3,2,1,0:T(8,128)(2,1)}) custom-call(s32[1]{0:T(128)S(6)} %copy.20.length, bf16[192,2,8,128]{3,2,1,0:T(8,128)(2,1)} %bitcast.18, bf16[192,2,8,128]{3,2,1,0:T(8,128)(2,1)} %bitcast.19, ...), custom_call_target="tpu_custom_call" | custom-call | tf_op jit(solution)/shard_map/pallas_call | solution.py:556
  82.8 0.0 copy-start.1
  82.8 0.8 slice_bitcast_fusion
  83.6 0.6 copy.17
  84.2 0.6 copy.16
  84.8 1.0 %fusion = (bf16[1,192,2,128]{3,1,0,2:T(8,128)(2,1)S(1)}, bf16[1,192,2,128]{3,1,0,2:T(8,128)(2,1)S(1)}) fusion(bf16[2,192,2,128]{3,1,0,2:T(8,128)(2,1)} %bitcast.20), kind=kLoop, calls=%fused_computation.3 | loop fusion | bytes 393216 | tf_op jit(solution)/shard_map/slice | solution.py:631
  85.8 0.7 copy.15
  86.5 0.7 copy.14
  87.3 0.0 copy-done.1
  87.3 0.0 copy-start
  87.3 0.9 copy.21
  88.1 0.5 copy-done
  88.7 0.9 copy.22
Async XLA Ops:
  82.8 4.5 %copy-start.1 = (bf16[192,2,8,128]{3,2,1,0:T(8,128)(2,1)S(1)}, bf16[192,2,8,128]{3,2,1,0:T(8,128)(2,1)}, u32[]{:S(2)}) copy-start(bf16[192,2,8,128]{3,2,1,0:T(8,128)(2,1)} %get-tuple-element.10) | copy-start | bytes 2359300
  87.3 1.4 %copy-start = (bf16[192,2,8,128]{3,2,1,0:T(8,128)(2,1)S(1)}, bf16[192,2,8,128]{3,2,1,0:T(8,128)(2,1)}, u32[]{:S(2)}) copy-start(bf16[192,2,8,128]{3,2,1,0:T(8,128)(2,1)} %get-tuple-element.11) | copy-start | bytes 2359300

commit v8 on v7

--- a/solution.py
+++ b/solution.py
@@ -89,7 +89,7 @@
 
 def kernel(
     length, q_in, do_in, kvp_in,
-    out, dq, dkv_out, dp_out,
+    out, dq, grads_out,
     raw, q2, do2, kv, acc, mx, tot, lse, off, o16, dk, dv, g16,
     zr, yrp, gyp, zrp, gx, gxp, xr, xrp,
     lsem, kvxs, kvxr, kvzs, kvzr, ppxs, ppxr, ppzs, ppzr, ppys, ppyr, qsem, osem,
@@ -191,25 +191,25 @@
         pz_copy((z + d) % 4).start()
 
     py_copy(z).start()
-    own_kv.wait()
-
-    @pl.loop(0, top + 1)
-    def _(tile):
-        @pl.when(tile != x)
-        def _():
-            remote(kv_in.at[hs], kv_rows(4 * tile + z), kvxs.at[tile], kvxr.at[tile], seq=4 * tile + z).wait_recv()
-
-        @pl.loop(1, 4)
-        def _(d):
-            @pl.when(uses((z + d) % 4, tile, z))
-            def _():
-                kvz_copy((z + d) % 4, tile).start()
-
     @pl.loop(1, 4)
     def _(d):
         zz = (z + d) % 4
         remote(p_column(r, zz), p_column(r, zz), ppzs.at[zz], ppzr.at[zz], seq=4 * x + zz).wait_recv()
         py_copy(zz).start()
+
+    own_kv.wait()
+
+    @pl.loop(0, top + 1)
+    def _(tile):
+        @pl.when(tile != x)
+        def _():
+            remote(kv_in.at[hs], kv_rows(4 * tile + z), kvxs.at[tile], kvxr.at[tile], seq=4 * tile + z).wait_recv()
+
+        @pl.loop(1, 4)
+        def _(d):
+            @pl.when(uses((z + d) % 4, tile, z))
+            def _():
+                kvz_copy((z + d) % 4, tile).start()
 
     do_out = remote(do_in.at[:, 1 - hs], raw.at[1, 1], qsem.at[2], qsem.at[3], seq=partner)
     do_out.start()
@@ -299,6 +299,15 @@
             def _():
                 gz_copy((z + d) % 4, tile).start()
 
+    def send_half(tile, half):
+        finish_rows(PRM + tile * TILE + half * HALF, HALF)
+
+        @pl.loop(2 * half, 2 * half + 2)
+        def _(zz):
+            @pl.when((zz != z) & gives(z, tile, zz))
+            def _():
+                gz_copy(zz, tile).start()
+
     def pass_tile(tile):
         rows = grad_rows(4 * tile + z)
         total = g16[:, rows, :].astype(f32)
@@ -451,14 +460,21 @@
         def _():
             backward_tile(b, 0, PRM, False)
 
-        @pl.when(kind == B_FULL)
-        def _():
-            def after(c):
-                @pl.when(has(DQ))
-                def _():
-                    send_dq(b, c)
-
-            backward_tile(b, PRM + tile * TILE, TILE, False, after)
+        @pl.when((kind == B_FULL) & jnp.logical_not(has(SEND) & has(DQ)))
+        def _():
+            backward_tile(b, PRM + tile * TILE, TILE, False)
+
+        @pl.when((kind == B_FULL) & has(SEND) & has(DQ))
+        def _():
+            @pl.loop(0, 2)
+            def _(half):
+                def after(c):
+                    @pl.when(half == 1)
+                    def _():
+                        send_dq(b, c)
+
+                backward_tile(b, PRM + tile * TILE + half * HALF, HALF, False, after)
+                send_half(tile, half)
 
         @pl.when(kind == B_DIAG)
         def _():
@@ -466,12 +482,16 @@
             def _(half):
                 backward_tile(b, PRM + tile * TILE + half * HALF, HALF, True)
 
+                @pl.when(has(SEND) & has(DQ))
+                def _():
+                    send_half(tile, half)
+
             @pl.when(has(DQ))
             def _():
                 for c in range(RB // RC):
                     send_dq(b, c)
 
-        @pl.when(has(SEND))
+        @pl.when(has(SEND) & jnp.logical_not(has(DQ)))
         def _():
             send_tile(tile)
 
@@ -494,7 +514,9 @@
         remote(gxp.at[:, pl.ds(0, 32), :], xrp.at[xx], gpxs.at[xx], gpxr.at[xx], seq=4 * xx + z).wait_recv()
 
     for h in range(2):
-        dp_out[h] = (xrp[2 * h].astype(f32) + xrp[2 * h + 1].astype(f32)).astype(bf16)
+        total = (xrp[2 * h].astype(f32) + xrp[2 * h + 1].astype(f32)).astype(bf16)
+        grads_out[h, BLK : BLK + 32] = total[0]
+        grads_out[h, 2 * BLK + 32 :] = total[1]
 
     @pl.loop(1, 4)
     def _(d):
@@ -508,7 +530,8 @@
         total = jnp.zeros(xr.shape[1:], f32)
         for xx in (2 * h, 2 * h + 1):
             total = total + jnp.where(x <= max(xx, 3 - xx), xr[xx].astype(f32), 0.0)
-        dkv_out[h] = total.astype(bf16)
+        grads_out[h, :BLK] = total[0].astype(bf16)
+        grads_out[h, BLK + 32 : 2 * BLK + 32] = total[1].astype(bf16)
 
     py_copy(z).wait_send()
     gpy_out.wait_send()
@@ -558,11 +581,10 @@
         out_shape=[
             jax.ShapeDtypeStruct((BLK, 2, PG, HD), bf16),
             jax.ShapeDtypeStruct((BLK, 2, PG, HD), bf16),
-            jax.ShapeDtypeStruct((2, 2, BLK, HD), bf16),
-            jax.ShapeDtypeStruct((2, 2, 32, HD), bf16),
+            jax.ShapeDtypeStruct((2, 2 * (BLK + 32), HD), bf16),
         ],
         in_specs=[pl.BlockSpec(memory_space=pltpu.SMEM)] + [any_spec] * 3,
-        out_specs=[any_spec, any_spec, vmem, vmem],
+        out_specs=[any_spec, any_spec, vmem],
         scratch_shapes=[
             pltpu.VMEM((2, 2, BLK, PG, HD), bf16),
             pltpu.VMEM((2, RB, HD), bf16),
@@ -615,22 +637,63 @@
     )(lengths, q_rows, do_rows, kvp_rows)
 
 
+def output_kernel(out_in, dq_in, grads, out, dq, d_keys, d_values, d_prompt_keys, d_prompt_values, held, sem):
+    pieces = [
+        (source.at[rows], held.at[n, rows], target.at[rows])
+        for rows in (pl.ds(0, BLK // 2), pl.ds(BLK // 2, BLK // 2))
+        for n, (source, target) in enumerate(((out_in, out), (dq_in, dq)))
+    ]
+    loads = [pltpu.make_async_copy(a, b, sem.at[0, i]) for i, (a, b, _) in enumerate(pieces)]
+    stores = [pltpu.make_async_copy(b, c, sem.at[1, i]) for i, (_, b, c) in enumerate(pieces)]
+    for load in loads:
+        load.start()
+    for load, store in zip(loads, stores):
+        load.wait()
+        store.start()
+    first = 0
+    for target in (d_keys, d_prompt_keys, d_values, d_prompt_values):
+        count = target.shape[0]
+        for h in range(2):
+            target[:, h, :] = grads[h, first : first + count, :]
+        first += count
+    for store in stores:
+        store.wait()
+
+
+def write_outputs(out, dq, grads):
+    any_spec = pl.BlockSpec(memory_space=pl.ANY)
+    vmem = pl.BlockSpec(memory_space=pltpu.VMEM)
+    rows = jax.ShapeDtypeStruct((BLK, 2, PG, HD), bf16)
+    keys = jax.ShapeDtypeStruct((BLK, 2, HD), bf16)
+    prompt = jax.ShapeDtypeStruct((32, 2, HD), bf16)
+    return pl.pallas_call(
+        output_kernel,
+        out_shape=[rows, rows, keys, keys, prompt, prompt],
+        in_specs=[any_spec, any_spec, vmem],
+        out_specs=[any_spec, any_spec, vmem, vmem, vmem, vmem],
+        scratch_shapes=[
+            pltpu.VMEM((2, BLK, 2, PG, HD), bf16),
+            pltpu.SemaphoreType.DMA((2, 4)),
+        ],
+        compiler_params=pltpu.CompilerParams(vmem_limit_bytes=58 * 2**20),
+    )(out, dq, grads)
+
+
 def local(queries, rollout_keys, rollout_values, prompt_keys, prompt_values, grad_out, lengths):
     by_group = (BLK, 2, PG, HD)
     q_rows = queries.reshape(by_group)
     do_rows = grad_out.reshape(by_group)
     joined = jnp.concatenate([rollout_keys[0], prompt_keys, rollout_values[0], prompt_values])
     joined = lax.optimization_barrier(joined).reshape(2, BLK + 32, 2, HD)
-    out, dq, dkv, dprompt = attention(lengths, q_rows, do_rows, joined.transpose(2, 0, 1, 3))
-    dkv = dkv.transpose(1, 2, 0, 3)
-    dprompt = dprompt.transpose(1, 2, 0, 3)
+    out, dq, grads = attention(lengths, q_rows, do_rows, joined.transpose(2, 0, 1, 3))
+    out, dq, d_keys, d_values, d_prompt_keys, d_prompt_values = write_outputs(out, dq, grads)
     return (
         out.reshape(queries.shape),
         dq.reshape(queries.shape),
-        dkv[0][None],
-        dkv[1][None],
-        dprompt[0],
-        dprompt[1],
+        d_keys[None],
+        d_values[None],
+        d_prompt_keys,
+        d_prompt_values,
     )
 
 

time: 89.8 us -> 85.9 us (0.957)
  local copies, waits for them, and re-layouts: 7.51 us -> 0.72 us
  Pallas kernels: 79.4 us -> 82.4 us
    unnamed x10 -> x0, local copies, waits for them, and re-layouts: 5.02 us -> none
    pallas_call x0 -> x1, Pallas kernels: none -> 3.81 us  [write_outputs(): pl.pallas_call(output_kernel, out_shape=[rows, rows, keys, keys, prompt,...]
    slice x1 -> x0, local copies, waits for them, and re-layouts: 0.95 us -> none  [local(): dkv[1][None]]
where the time goes in v8:
time: 85.9 us; the launch traced here: 85.7 us
  Pallas kernels  82.4 us (96%)
  other arithmetic  1.32 us (2%)
  between operations  1.29 us (2%)
    pallas_call x1, Pallas kernels, attention(): pl.pallas_call(kernel, out_shape=[jax.ShapeDtypeStruct((BLK, 2, PG, HD),...  78.6 us
    pallas_call x1, Pallas kernels, write_outputs(): pl.pallas_call(output_kernel, out_shape=[rows, rows, keys, keys, prompt,...  3.81 us

profile of v8, /device:TPU:0, one launch (start us, length us, event | category | flops | bytes accessed | tf_op | source)
XLA Modules:
  0.0 85.7 jit_solution(10634637297467517509)
XLA Ops:
  1.3 1.3 %pad_maximum_fusion = bf16[448,2,128]{2,1,0:T(2,128)(2,1)S(1)} fusion(bf16[32,2,128]{2,1,0:T(2,128)(2,1)} %param.11, bf16[192,2,128]{2,1,0:T(2,128)(2,1)} %bitcast.14, bf16[32,2,128]{2,1,0:T(2,128)(2,1)} %param.10, bf16[192,2,128]{2,1,0:T(2,128)(2,1)} %bitcast.15), kind=kLoop, calls=%fused_computation | loop fusion | flops 344064 | bytes 458752 | tf_op jit(solution)/shard_map/concatenate | solution.py:686
  2.6 0.7 copy.13
  3.3 78.6 %shard_map.118 = (bf16[192,2,8,128]{3,2,1,0:T(8,128)(2,1)}, bf16[192,2,8,128]{3,2,1,0:T(8,128)(2,1)}, bf16[2,448,128]{2,1,0:T(8,128)(2,1)}) custom-call(s32[1]{0:T(128)S(6)} %copy.14.length, bf16[192,2,8,128]{3,2,1,0:T(8,128)(2,1)} %bitcast.12, bf16[192,2,8,128]{3,2,1,0:T(8,128)(2,1)} %bitcast.13, bf16[2,2,224,128]{3,2,1,0:T(8,128)(2,1)} %bitcast.11), custom_call_target="tpu_custom_call" | custom-call | tf_op jit(solution)/shard_map/pallas_call | solution.py:579
  81.9 3.8 %shard_map.119 = (bf16[192,2,8,128]{3,2,1,0:T(8,128)(2,1)}, bf16[192,2,8,128]{3,2,1,0:T(8,128)(2,1)}, bf16[192,2,128]{2,1,0:T(2,128)(2,1)}, bf16[192,2,128]{2,1,...) custom-call(bf16[192,2,8,128]{3,2,1,0:T(8,128)(2,1)} %get-tuple-element.15.out_in, ...), custom_call_target="tpu_custom_call" | custom-call | tf_op jit(solution)/shard_map/pallas_call | solution.py:669

commit v9 on v8

--- a/solution.py
+++ b/solution.py
@@ -637,7 +637,9 @@
     )(lengths, q_rows, do_rows, kvp_rows)
 
 
-def output_kernel(out_in, dq_in, grads, out, dq, d_keys, d_values, d_prompt_keys, d_prompt_values, held, sem):
+def output_kernel(out_in, dq_in, grads, out, dq, d_keys, d_values, d_prompt_keys, d_prompt_values, held, g_held, k_held, pk_held, v_held, pv_held, sem, gsem):
+    load_g = pltpu.make_async_copy(grads, g_held, gsem.at[4])
+    load_g.start()
     pieces = [
         (source.at[rows], held.at[n, rows], target.at[rows])
         for rows in (pl.ds(0, BLK // 2), pl.ds(BLK // 2, BLK // 2))
@@ -650,30 +652,40 @@
     for load, store in zip(loads, stores):
         load.wait()
         store.start()
+    load_g.wait()
     first = 0
-    for target in (d_keys, d_prompt_keys, d_values, d_prompt_values):
+    parts = ((k_held, d_keys), (v_held, d_values), (pk_held, d_prompt_keys), (pv_held, d_prompt_values))
+    for n, (kept, target) in enumerate((parts[0], parts[2], parts[1], parts[3])):
         count = target.shape[0]
         for h in range(2):
-            target[:, h, :] = grads[h, first : first + count, :]
+            kept[:, h, :] = g_held[h, first : first + count, :]
         first += count
+        store = pltpu.make_async_copy(kept, target, gsem.at[n])
+        store.start()
+        stores.append(store)
     for store in stores:
         store.wait()
 
 
 def write_outputs(out, dq, grads):
     any_spec = pl.BlockSpec(memory_space=pl.ANY)
-    vmem = pl.BlockSpec(memory_space=pltpu.VMEM)
     rows = jax.ShapeDtypeStruct((BLK, 2, PG, HD), bf16)
     keys = jax.ShapeDtypeStruct((BLK, 2, HD), bf16)
     prompt = jax.ShapeDtypeStruct((32, 2, HD), bf16)
     return pl.pallas_call(
         output_kernel,
         out_shape=[rows, rows, keys, keys, prompt, prompt],
-        in_specs=[any_spec, any_spec, vmem],
-        out_specs=[any_spec, any_spec, vmem, vmem, vmem, vmem],
+        in_specs=[any_spec] * 3,
+        out_specs=[any_spec] * 6,
         scratch_shapes=[
             pltpu.VMEM((2, BLK, 2, PG, HD), bf16),
+            pltpu.VMEM((2, 2 * (BLK + 32), HD), bf16),
+            pltpu.VMEM((BLK, 2, HD), bf16),
+            pltpu.VMEM((32, 2, HD), bf16),
+            pltpu.VMEM((BLK, 2, HD), bf16),
+            pltpu.VMEM((32, 2, HD), bf16),
             pltpu.SemaphoreType.DMA((2, 4)),
+            pltpu.SemaphoreType.DMA((5,)),
         ],
         compiler_params=pltpu.CompilerParams(vmem_limit_bytes=58 * 2**20),
     )(out, dq, grads)

time: 85.9 us -> 85 us (0.990)
  Pallas kernels: 82.4 us -> 81.5 us
    pallas_call x1, Pallas kernels: 3.81 us -> 2.9 us  [write_outputs(): pl.pallas_call(output_kernel, out_shape=[rows, rows, keys, keys, prompt,...]
where the time goes in v9:
time: 85 us; the launch traced here: 84.8 us
  Pallas kernels  81.5 us (96%)
  other arithmetic  1.32 us (2%)
  between operations  1.29 us (2%)
    pallas_call x1, Pallas kernels, attention(): pl.pallas_call(kernel, out_shape=[jax.ShapeDtypeStruct((BLK, 2, PG, HD),...  78.6 us
    pallas_call x1, Pallas kernels, write_outputs(): pl.pallas_call(output_kernel, out_shape=[rows, rows, keys, keys, prompt,...  2.9 us

profile of v9, /device:TPU:0, one launch (start us, length us, event | category | flops | bytes accessed | tf_op | source)
XLA Modules:
  0.0 84.8 jit_solution(17060625861506609089)
XLA Ops:
  1.3 1.3 %pad_maximum_fusion = bf16[448,2,128]{2,1,0:T(2,128)(2,1)S(1)} fusion(bf16[32,2,128]{2,1,0:T(2,128)(2,1)} %param.11, bf16[192,2,128]{2,1,0:T(2,128)(2,1)} %bitcast.14, bf16[32,2,128]{2,1,0:T(2,128)(2,1)} %param.10, bf16[192,2,128]{2,1,0:T(2,128)(2,1)} %bitcast.15), kind=kLoop, calls=%fused_computation | loop fusion | flops 344064 | bytes 458752 | tf_op jit(solution)/shard_map/concatenate | solution.py:698
  2.6 0.7 copy.13
  3.3 78.6 %shard_map.118 = (bf16[192,2,8,128]{3,2,1,0:T(8,128)(2,1)}, bf16[192,2,8,128]{3,2,1,0:T(8,128)(2,1)}, bf16[2,448,128]{2,1,0:T(8,128)(2,1)}) custom-call(s32[1]{0:T(128)S(6)} %copy.14.length, bf16[192,2,8,128]{3,2,1,0:T(8,128)(2,1)} %bitcast.12, bf16[192,2,8,128]{3,2,1,0:T(8,128)(2,1)} %bitcast.13, bf16[2,2,224,128]{3,2,1,0:T(8,128)(2,1)} %bitcast.11), custom_call_target="tpu_custom_call" | custom-call | tf_op jit(solution)/shard_map/pallas_call | solution.py:579
  81.9 2.9 %shard_map.119 = (bf16[192,2,8,128]{3,2,1,0:T(8,128)(2,1)}, bf16[192,2,8,128]{3,2,1,0:T(8,128)(2,1)}, bf16[192,2,128]{2,1,0:T(2,128)(2,1)}, bf16[192,2,128]{2,1,...) custom-call(bf16[192,2,8,128]{3,2,1,0:T(8,128)(2,1)} %get-tuple-element.15.out_in, ...), custom_call_target="tpu_custom_call" | custom-call | tf_op jit(solution)/shard_map/pallas_call | solution.py:675
